TPU v7x, 32 devices: a whole 2x2x4 slice. The times are simulated.
32 devices in a mesh: mic: 8 (over y, x, core), tile: 4 (over z).
Axes of the slice: x: 2, y: 2, z: 4, core: 2. Of those that a mesh axis runs over, the one named last changes fastest.
Arguments:
- micrograph: bfloat16 [8, 447, 1536], P('mic', None, 'tile'), may hold values from -6 to 6
- templates: bfloat16 [8, 384, 384], P('mic'), may hold values from -6 to 6
- orient_ids: int32 [8], P('mic'), may hold values from 0 to 359
- defocus_bins: int32 [8], P('mic'), may hold values from 0 to 15
Outputs:
- peak_value: float32 [8, 64, 1536], P('mic', None, 'tile')
- corr_sum: float32 [8, 64, 1536], P('mic', None, 'tile')
- corr_sumsq: float32 [8, 64, 1536], P('mic', None, 'tile')
- orient_cos: float32 [8, 64, 1536], P('mic', None, 'tile')
- orient_sin: float32 [8, 64, 1536], P('mic', None, 'tile')
All inputs are finite; a program needn't handle non-finite values.
Results may differ from a plain program's by a relative error of at most 0.013.
Values may be sent and summed in bfloat16 or wider, within the bound.
No kernel may reach another device: no remote copies, remote signals or barrier semaphores. Data moves between devices by JAX's collectives and lax.ppermute only.
A program may use at most 64 MiB of HBM per device.

v0:
```python
import math

import jax
import jax.numpy as jnp
from jax import lax
from jax.sharding import PartitionSpec as P

TS = 384
TC = 384
MH = 64
STEPS = 4
NANG = 360
MR = 447
MC = 767
LR = 448
LC = 768
HALF = 384


AMPLITUDE = 0.07
WAVELENGTH = 0.0197
BASE_DEFOCUS = 8000.0
DEFOCUS_STEP = 1000.0


def from_behind(array, axis, by):
    count = lax.axis_size(axis)
    pairs = [(i, i + by) for i in range(count) if 0 <= i + by < count]
    return lax.ppermute(array, axis, pairs)


def passed_along(array, axis, by):
    count = lax.axis_size(axis)
    return lax.ppermute(array, axis, [(i, (i + by) % count) for i in range(count)])


def counting(length):
    return jnp.arange(length, dtype=jnp.int32)


def trig_pair(left_ids, right_ids, length):
    product_ids = left_ids[:, None] * right_ids[None, :] % length
    angles = product_ids.astype(jnp.float32) * (2.0 * math.pi / length)
    return (jnp.cos(angles).astype(jnp.bfloat16), jnp.sin(angles).astype(jnp.bfloat16))


def forward_columns(height, breadth, length):
    cosine, sine_part = trig_pair(counting(height), counting(breadth), length)
    return jnp.concatenate([cosine, -sine_part], axis=1)


def inverse_columns(breadth, height, length):
    cosine, sine_part = trig_pair(counting(breadth), counting(height), length)
    weights = jnp.where(counting(breadth) == 0, 1.0, 2.0).astype(jnp.bfloat16)[:, None]
    return jnp.concatenate([cosine * weights, -sine_part * weights], axis=0)


def stacked_rows(left_ids, right_ids, length):
    cosine, sine_part = trig_pair(left_ids, right_ids, length)
    return jnp.concatenate([cosine, sine_part], axis=0)


def complex_left(stacked, values, direction):
    product = jnp.dot(stacked, values, preferred_element_type=jnp.float32)
    height = stacked.shape[0] // 2
    breadth = values.shape[1] // 2
    upper_part = product[:height]
    lower_part = product[height:]
    real_part = upper_part[:, :breadth] - direction * lower_part[:, breadth:]
    imag_part = upper_part[:, breadth:] + direction * lower_part[:, :breadth]
    return jnp.concatenate([real_part, imag_part], axis=1)


def transfer_function(bin_value, rows_length, breadth, cols_length):
    row_ids = counting(rows_length)
    folded = (row_ids + rows_length // 2) % rows_length - rows_length // 2
    freq_rows = folded.astype(jnp.float32) / rows_length
    freq_cols = counting(breadth).astype(jnp.float32) / cols_length
    radius = freq_rows[:, None] * freq_rows[:, None] + freq_cols[None, :] * freq_cols[None, :]
    defocus = BASE_DEFOCUS + DEFOCUS_STEP * bin_value.astype(jnp.float32)
    phases = math.pi * WAVELENGTH * defocus * radius
    return -(math.sqrt(1.0 - AMPLITUDE * AMPLITUDE) * jnp.sin(phases) + AMPLITUDE * jnp.cos(phases))


def angle_pairs(orient_ids):
    angles = orient_ids.astype(jnp.float32) * (2.0 * math.pi / NANG)
    return jnp.stack([jnp.cos(angles), jnp.sin(angles)], axis=-1).astype(jnp.bfloat16)


def micro_spectrum(micro_strip, col_forward, row_forward, ctf_values):
    spectrum_cols = jnp.dot(micro_strip, col_forward, preferred_element_type=jnp.float32).astype(
        jnp.bfloat16
    )
    spectrum = complex_left(row_forward, spectrum_cols, -1.0)
    return (spectrum * jnp.concatenate([ctf_values, ctf_values], axis=1)).astype(jnp.bfloat16)


def spectral_product(micro_rows, template_rows):
    breadth = micro_rows.shape[1] // 2
    micro_real = micro_rows[:, :breadth].astype(jnp.float32)
    micro_imag = micro_rows[:, breadth:].astype(jnp.float32)
    tmpl_real = template_rows[:, :breadth].astype(jnp.float32)
    tmpl_imag = template_rows[:, breadth:].astype(jnp.float32)
    real_part = micro_real * tmpl_real + micro_imag * tmpl_imag
    imag_part = micro_imag * tmpl_real - micro_real * tmpl_imag
    return jnp.concatenate([real_part, imag_part], axis=1).astype(jnp.bfloat16)


def accumulate(statistics, correlation, angle_pair):
    weight = jax.nn.softplus(2.0 * correlation)
    cos_value = angle_pair[0].astype(jnp.float32)
    sin_value = angle_pair[1].astype(jnp.float32)
    fresh = (
        correlation,
        correlation,
        correlation * correlation,
        weight,
        weight * cos_value,
        weight * sin_value,
    )
    if statistics is None:
        return fresh
    return (
        jnp.maximum(statistics[0], fresh[0]),
        statistics[1] + fresh[1],
        statistics[2] + fresh[2],
        statistics[3] + fresh[3],
        statistics[4] + fresh[4],
        statistics[5] + fresh[5],
    )


def finish(statistics):
    return (
        statistics[0],
        statistics[1],
        statistics[2],
        statistics[4] / statistics[3],
        statistics[5] / statistics[3],
    )


def body(micrograph, templates, orient_ids, defocus_bins):
    own_strip = micrograph[0]
    halo_cells = from_behind(own_strip[:, : TS - 1], "tile", -1)
    micro_strip = jnp.concatenate([own_strip, halo_cells], axis=1)
    col_forward = forward_columns(MC, HALF, LC)
    row_forward = stacked_rows(counting(LR), counting(MR), LR)
    row_inverse = stacked_rows(counting(MH), counting(LR), LR)
    col_inverse = inverse_columns(HALF, TC, LC)
    norm_scale = 1.0 / (TS * LR * LC)
    ctf_values = transfer_function(defocus_bins[0], LR, HALF, LC)
    micro_spec = micro_spectrum(micro_strip, col_forward, row_forward, ctf_values)
    own_angle = angle_pairs(orient_ids)[0]
    template_forward = col_forward[:TS]

    def column_rows(rows_piece):
        return jnp.dot(rows_piece, template_forward, preferred_element_type=jnp.float32).astype(
            jnp.bfloat16
        )

    row_template = stacked_rows(counting(LR), counting(TS), LR)
    current = templates[0]
    angle_now = own_angle
    statistics = None
    for step_index in range(STEPS):
        if step_index == 0:
            template_cols = column_rows(templates[0])
        else:
            template_cols = column_rows(current)
        template_spec = complex_left(row_template, template_cols, -1.0).astype(jnp.bfloat16)
        inverse_rows = complex_left(
            row_inverse, spectral_product(micro_spec, template_spec), 1.0
        ).astype(jnp.bfloat16)
        correlation = (
            jnp.dot(inverse_rows, col_inverse, preferred_element_type=jnp.float32) * norm_scale
        )
        statistics = accumulate(statistics, correlation, angle_now)
        if step_index + 1 < STEPS:
            current, angle_now = passed_along((current, angle_now), "mic", -1)
    results = finish(statistics)
    return (
        results[0][None],
        results[1][None],
        results[2][None],
        results[3][None],
        results[4][None],
    )


def solution(mesh):
    placed = (P("mic", None, "tile"), P("mic", None, None), P("mic"), P("mic"))
    return jax.shard_map(
        body,
        mesh=mesh,
        in_specs=placed,
        out_specs=(
            P("mic", None, "tile"),
            P("mic", None, "tile"),
            P("mic", None, "tile"),
            P("mic", None, "tile"),
            P("mic", None, "tile"),
        ),
        check_vma=False,
    )
```

profile of v0, /device:TPU:27, one launch (start us, length us, event | category | flops | bytes accessed | tf_op | source)
XLA Modules:
  0.0 84.0 jit_solution(1967921768599427259)
XLA Ops:
  0.6 2.8 %collective-permute-start = (bf16[447,383]{1,0:T(8,128)(2,1)}, bf16[447,383]{1,0:T(8,128)(2,1)}, u32[]{:S(2)}, u32[]{:S(2)}) collective-permute-start(bf16[447,383]{1,0:T(8,128)(2,1)} %bitcast.41), channel_id=1, source_target_pairs={{1,0},{2,1},{3,2},{5,4},{6,5},{7,6},{9,8},{10,9},{11,10},{13,12},{... | collective-permute-start | bytes 1027214 | tf_op jit(solution)/shard_map/ppermute | solution.py:29
  3.5 1.0 %collective-permute-start.1 = (bf16[384,384]{1,0:T(8,128)(2,1)}, bf16[384,384]{1,0:T(8,128)(2,1)}, u32[]{:S(2)}, u32[]{:S(2)}) collective-permute-start(bf16[384,384]{1,0:T(8,128)(2,1)} %bitcast.40), channel_id=1, source_target_pairs={{0,28},{4,0},{8,4},{12,8},{16,12},{20,16},{24,20},{28,24},{1,29},{... | collective-permute-start | bytes 884744 | tf_op jit(solution)/shard_map/ppermute | solution.py:34
  5.2 0.1 pad_maximum_fusion.4
  5.3 0.0 collective-permute-start.4
  5.3 4.9 %sine_convert_fusion.1 = (bf16[448,447]{1,0:T(8,128)(2,1)}, bf16[448,447]{1,0:T(8,128)(2,1)}) fusion(), kind=kLoop, calls=%fused_computation.47 | loop fusion | flops 2202816 | bytes 801024 | tf_op jit(solution)/shard_map/convert_element_type | solution.py:44
  10.2 4.6 %cosine_convert_fusion = bf16[767,384]{1,0:T(8,128)(2,1)S(1)} fusion(), kind=kLoop, calls=%fused_computation.36 | loop fusion | flops 2945280 | bytes 589056 | tf_op jit(solution)/shard_map/convert_element_type | solution.py:44
  14.8 4.7 %fusion.88 = bf16[767,384]{1,0:T(8,128)(2,1)S(1)} fusion(), kind=kLoop, calls=%fused_computation.129 | loop fusion | flops 3828864 | bytes 589056 | tf_op jit(solution)/shard_map/neg | solution.py:49
  19.5 3.0 %sine_convert_fusion.2 = (bf16[448,384]{1,0:T(8,128)(2,1)S(1)}, bf16[448,384]{1,0:T(8,128)(2,1)S(1)}) fusion(), kind=kLoop, calls=%fused_computation.120 | loop fusion | flops 1892352 | bytes 688128 | tf_op jit(solution)/shard_map/convert_element_type | solution.py:44
  22.5 1.2 %sine_convert_fusion.4 = (bf16[64,448]{1,0:T(8,128)(2,1)S(1)}, bf16[64,448]{1,0:T(8,128)(2,1)}) fusion(), kind=kLoop, calls=%fused_computation.149 | loop fusion | flops 315392 | bytes 114688 | tf_op jit(solution)/shard_map/convert_element_type | solution.py:44
  24.3 3.3 %fusion.92 = (bf16[384,384]{1,0:T(8,128)(2,1)}, bf16[384,384]{1,0:T(8,128)(2,1)}) fusion(bf16[384]{0:T(512)(128)(2,1)S(1)} %select_convert_fusion), kind=kLoop, calls=%fused_computation.138 | loop fusion | flops 2801664 | bytes 590592 | tf_op jit(solution)/shard_map/mul | solution.py:55
  27.7 2.6 %add_negate_fusion = f32[448,384]{1,0:T(8,128)S(1)} fusion(f32[384]{0:T(512)S(1)} %multiply_multiply_fusion, f32[448]{0:T(512)S(1)} %fusion.127, f32[]{:T(128)} %bitcast.1), kind=kLoop, calls=%fused_computation.125 | loop fusion | flops 1032192 | bytes 691460 | tf_op jit(solution)/shard_map/neg | solution.py:82
  30.3 3.0 %fusion.2 = f32[896,768]{1,0:T(8,128)} fusion(bf16[384,768]{1,0:T(8,128)(2,1)S(1)} %pad_maximum_fusion.1, bf16[1,384,384]{2,1,0:T(8,128)(2,1)S(1)} %copy-done.2, bf16[448,384]{1,0:T(8,128)(2,1)S(1)} %get-tuple-element.48, bf16[448,384]{1,0:T(8,128)(2,1)S(1)} %get-tuple-element.49), kind=kOutput, calls=%fused_computation.26 | convolution fusion | flops 756645888 | bytes 4325376 | tf_op jit(solution)/shard_map/dot_general | solution.py:64
  33.3 0.6 fusion.151
  35.2 0.7 collective-permute-start.5
  35.9 3.2 %collective-permute-done.5 = bf16[2]{0:T(256)(128)(2,1)S(1)} collective-permute-done((bf16[2]{0:T(256)(128)(2,1)S(1)}, bf16[2]{0:T(256)(128)(2,1)S(1)}, u32[]{:S(2)}, u32[]{:S(2)}) %collective-permute-start.5) | collective-permute-done | bytes 36 | tf_op jit(solution)/shard_map/ppermute | solution.py:34
  39.2 0.6 fusion.152
  41.0 0.1 collective-permute-start.6
  41.1 3.9 %collective-permute-done.6 = bf16[2]{0:T(256)(128)(2,1)S(1)} collective-permute-done((bf16[2]{0:T(256)(128)(2,1)S(1)}, bf16[2]{0:T(256)(128)(2,1)S(1)}, u32[]{:S(2)}, u32[]{:S(2)}) %collective-permute-start.6) | collective-permute-done | bytes 36 | tf_op jit(solution)/shard_map/ppermute | solution.py:34
  45.0 0.6 fusion.153
  46.9 0.0 collective-permute-done.1
  46.9 0.2 collective-permute-start.2
  47.1 4.1 %fusion.3 = f32[896,768]{1,0:T(8,128)} fusion(bf16[384,768]{1,0:T(8,128)(2,1)S(1)} %pad_maximum_fusion.1, bf16[384,384]{1,0:T(8,128)(2,1)} %collective-permute-done.1, bf16[448,384]{1,0:T(8,128)(2,1)S(1)} %get-tuple-element.48, bf16[448,384]{1,0:T(8,128)(2,1)S(1)} %get-tuple-element.49), kind=kOutput, calls=%fused_computation.27 | convolution fusion | flops 756645888 | bytes 4325376 | tf_op jit(solution)/shard_map/dot_general | solution.py:64
  51.2 4.5 %fusion.1 = f32[896,768]{1,0:T(8,128)} fusion(bf16[767,384]{1,0:T(8,128)(2,1)S(1)} %fusion.88, bf16[767,384]{1,0:T(8,128)(2,1)S(1)} %cosine_convert_fusion, bf16[448,447]{1,0:T(8,128)(2,1)} %get-tuple-element.46, bf16[448,447]{1,0:T(8,128)(2,1)} %get-tuple-element.47, bf16[447,383]{1,0:T(8,128)(2,1)} %collective-permute-done, bf16[447,384]{1,0:T(8,128)(2,1)} %bitcast.42), kind=kOutput, calls=%fused_computation.25 | convolution fusion | flops 1147475456 | bytes 5417346 | tf_op jit(solution)/shard_map/dot_general | solution.py:64
  55.7 1.9 %fusion.60 = (f32[448,384]{1,0:T(8,128)S(1)}, f32[448,384]{1,0:T(8,128)S(1)}) fusion(f32[896,768]{1,0:T(8,128)} %fusion.1), kind=kLoop, calls=%fused_computation.99 | loop fusion | flops 688128 | bytes 4128768 | tf_op jit(solution)/shard_map/sub | solution.py:69
  57.5 0.2 fusion
  57.7 0.0 collective-permute-done.2
  57.7 3.1 %fusion.4 = f32[896,768]{1,0:T(8,128)} fusion(bf16[384,768]{1,0:T(8,128)(2,1)S(1)} %pad_maximum_fusion.1, bf16[384,384]{1,0:T(8,128)(2,1)S(1)} %collective-permute-done.2, bf16[448,384]{1,0:T(8,128)(2,1)S(1)} %get-tuple-element.48, bf16[448,384]{1,0:T(8,128)(2,1)S(1)} %get-tuple-element.49), kind=kOutput, calls=%fused_computation.28 | convolution fusion | flops 756645888 | bytes 4325376 | tf_op jit(solution)/shard_map/dot_general | solution.py:64
  60.8 3.2 %fusion.32 = (bf16[448,384]{1,0:T(8,128)(2,1)S(1)}, bf16[448,384]{1,0:T(8,128)(2,1)S(1)}, bf16[448,384]{1,0:T(8,128)(2,1)S(1)}, bf16[448,384]{1,0:T(8,128)(2,1)S...) fusion(bf16[448,768]{1,0:T(8,128)(2,1)S(1)} %fusion, f32[896,768]{1,0:T(8,128)} %fusion.3, ...), kind=kLoop, calls=%fused_computation.61 | loop fusion | flops 4472832 | bytes 8257536 | tf_op jit(solution)/shard_map/convert.28
  64.0 0.2 copy-done
  64.3 1.2 %fusion.28 = (bf16[448,384]{1,0:T(8,128)(2,1)}, bf16[448,384]{1,0:T(8,128)(2,1)S(1)}, bf16[448,384]{1,0:T(8,128)(2,1)S(1)}, bf16[448,384]{1,0:T(8,128)(2,1)S(1)}, bf16[448,384]{1,0:T(8,128)(2,1)S(1)}) fusion(bf16[448,768]{1,0:T(8,128)(2,1)S(1)} %fusion, f32[896,768]{1,0:T(8,128)S(1)} %copy-done, bf16[448,384]{1,0:T(8,128)(2,1)S(1)} %get-tuple-element.23, ...), kind=kLoop, calls=%fused_computation.57 | loop fusion | flops 4472832 | bytes 6537216 | tf_op jit(solution)/shard_map/convert.34
  65.5 0.3 fusion.75
  65.8 0.3 fusion.71
  66.1 0.4 copy-done.5
  66.4 0.1 copy-done.7
  66.5 0.9 %fusion.116 = f32[64,384]{1,0:T(8,128)} fusion(bf16[64,384]{1,0:T(8,128)(2,1)S(1)} %get-tuple-element.35, bf16[64,384]{1,0:T(8,128)(2,1)S(1)} %get-tuple-element.34, bf16[384,384]{1,0:T(8,128)(2,1)S(1)} %copy-done.7, bf16[384,384]{1,0:T(8,128)(2,1)S(1)} %copy-done.5), kind=kOutput, calls=%fused_computation.179 | convolution fusion | flops 39124992 | bytes 786432 | tf_op jit(solution)/shard_map/dot_general | solution.py:176
  67.4 0.5 collective-permute-start.3
  67.9 0.2 fusion.112
  68.1 6.5 %collective-permute-done.3 = bf16[384,384]{1,0:T(8,128)(2,1)} collective-permute-done((bf16[384,384]{1,0:T(8,128)(2,1)S(1)}, bf16[384,384]{1,0:T(8,128)(2,1)}, u32[]{:S(2)}, u32[]{:S(2)}) %collective-permute-start.3) | collective-permute-done | bytes 294944 | tf_op jit(solution)/shard_map/ppermute | solution.py:34
  74.6 4.0 %fusion.5 = f32[896,768]{1,0:T(8,128)} fusion(bf16[384,768]{1,0:T(8,128)(2,1)S(1)} %pad_maximum_fusion.1, bf16[384,384]{1,0:T(8,128)(2,1)} %collective-permute-done.3, bf16[448,384]{1,0:T(8,128)(2,1)S(1)} %get-tuple-element.48, bf16[448,384]{1,0:T(8,128)(2,1)S(1)} %get-tuple-element.49), kind=kOutput, calls=%fused_computation.29 | convolution fusion | flops 756645888 | bytes 4325376 | tf_op jit(solution)/shard_map/dot_general | solution.py:64
  78.6 2.1 %fusion.40 = (bf16[448,384]{1,0:T(8,128)(2,1)S(1)}, bf16[448,384]{1,0:T(8,128)(2,1)S(1)}, bf16[448,384]{1,0:T(8,128)(2,1)S(1)}, bf16[448,384]{1,0:T(8,128)(2,1)S(1)}) fusion(bf16[448,768]{1,0:T(8,128)(2,1)S(1)} %fusion, f32[896,768]{1,0:T(8,128)} %fusion.5, bf16[448,384]{1,0:T(8,128)(2,1)S(1)} %get-tuple-element.7, bf16[448,384]{1,0:T(8,128)(2,1)S(1)} %get-tuple-element.6), kind=kLoop, calls=%fused_computation.69 | loop fusion | flops 3440640 | bytes 5505024 | tf_op jit(solution)/shard_map/convert.16
  80.7 0.2 fusion.42
  80.9 0.3 fusion.79
  81.2 0.6 copy-done.1
  81.9 0.3 fusion.67
  82.2 0.1 copy-done.8
  82.2 0.2 fusion.108
  82.5 0.3 copy-done.10
  82.8 1.3 %divide_bitcast_fusion = (f32[1,64,384]{2,1,0:T(8,128)}, f32[1,64,384]{2,1,0:T(8,128)}, f32[1,64,384]{2,1,0:T(8,128)}, f32[1,64,384]{2,1,0:T(8,128)}, f32[1,64,384]{2,1,0:T(8,128)}) fusion(f32[]{:T(128)S(6)} %convert.99, f32[]{:T(128)S(6)} %convert.98, f32[]{:T(128)S(6)} %convert.97, f32[]{:T(128)S(6)} %convert.96, f32[64,384]{1,0:T(8,128)S(1)} %fusion.108, ...), kind=kOutput, calls=%fused_computation.187 | convolution fusion | flops 40697856 | bytes 1474592 | tf_op jit(solution)/shard_map/dot_general | solution.py:176
  (26 shorter events, 0.2 us)
Async XLA Ops:
  0.6 50.5 %collective-permute-start = (bf16[447,383]{1,0:T(8,128)(2,1)}, bf16[447,383]{1,0:T(8,128)(2,1)}, u32[]{:S(2)}, u32[]{:S(2)}) collective-permute-start(bf16[447,383]{1,0:T(8,128)(2,1)} %bitcast.41), channel_id=1, source_target_pairs={{1,0},{2,1},{3,2},{5,4},{6,5},{7,6},{9,8},{10,9},{11,10},{13,12},{... | collective-permute-start | bytes 1027214 | tf_op jit(solution)/shard_map/ppermute | solution.py:29
  3.5 43.4 %collective-permute-start.1 = (bf16[384,384]{1,0:T(8,128)(2,1)}, bf16[384,384]{1,0:T(8,128)(2,1)}, u32[]{:S(2)}, u32[]{:S(2)}) collective-permute-start(bf16[384,384]{1,0:T(8,128)(2,1)} %bitcast.40), channel_id=1, source_target_pairs={{0,28},{4,0},{8,4},{12,8},{16,12},{20,16},{24,20},{28,24},{1,29},{... | collective-permute-start | bytes 884744 | tf_op jit(solution)/shard_map/ppermute | solution.py:34
  5.3 28.0 %collective-permute-start.4 = (bf16[2]{0:T(256)(128)(2,1)S(1)}, bf16[2]{0:T(256)(128)(2,1)S(1)}, u32[]{:S(2)}, u32[]{:S(2)}) collective-permute-start(bf16[2]{0:T(256)(128)(2,1)S(1)} %pad_maximum_fusion.4), channel_id=1, source_target_pairs={{0,28},{4,0},{8,4},{12,8},{16,12},{20,16},{24,20},{28,24},{1,29},{... | collective-permute-start | bytes 20 | tf_op jit(solution)/shard_map/ppermute | solution.py:34
  27.6 2.6 %copy-start.2 = (bf16[1,384,384]{2,1,0:T(8,128)(2,1)S(1)}, bf16[1,384,384]{2,1,0:T(8,128)(2,1)}, u32[]{:S(2)}) copy-start(bf16[1,384,384]{2,1,0:T(8,128)(2,1)} %param.5) | copy-start | bytes 884740
  35.2 3.9 %collective-permute-start.5 = (bf16[2]{0:T(256)(128)(2,1)S(1)}, bf16[2]{0:T(256)(128)(2,1)S(1)}, u32[]{:S(2)}, u32[]{:S(2)}) collective-permute-start(bf16[2]{0:T(256)(128)(2,1)S(1)} %collective-permute-done.4), channel_id=1, source_target_pairs={{0,28},{4,0},{8,4},{12,8},{16,12},{20,16},{24,20},{28,24},{1,29},{... | collective-permute-start | bytes 20 | tf_op jit(solution)/shard_map/ppermute | solution.py:34
  41.0 3.9 %collective-permute-start.6 = (bf16[2]{0:T(256)(128)(2,1)S(1)}, bf16[2]{0:T(256)(128)(2,1)S(1)}, u32[]{:S(2)}, u32[]{:S(2)}) collective-permute-start(bf16[2]{0:T(256)(128)(2,1)S(1)} %collective-permute-done.5), channel_id=1, source_target_pairs={{0,28},{4,0},{8,4},{12,8},{16,12},{20,16},{24,20},{28,24},{1,29},{... | collective-permute-start | bytes 20 | tf_op jit(solution)/shard_map/ppermute | solution.py:34
  46.9 10.8 %collective-permute-start.2 = (bf16[384,384]{1,0:T(8,128)(2,1)}, bf16[384,384]{1,0:T(8,128)(2,1)S(1)}, u32[]{:S(2)}, u32[]{:S(2)}) collective-permute-start(bf16[384,384]{1,0:T(8,128)(2,1)} %collective-permute-done.1), channel_id=1, source_target_pairs={{0,28},{4,0},{8,4},{12,8},{16,12},{20,16},{24,20},{28,24},{1,29},{... | collective-permute-start | bytes 884744 | tf_op jit(solution)/shard_map/ppermute | solution.py:34
  57.7 3.1 %copy-start.3 = (bf16[384,384]{1,0:T(8,128)(2,1)}, bf16[384,384]{1,0:T(8,128)(2,1)S(1)}, u32[]{:S(2)}) copy-start(bf16[384,384]{1,0:T(8,128)(2,1)S(1)} %collective-permute-done.2) | copy-start | bytes 884740
  60.8 3.4 %copy-start = (f32[896,768]{1,0:T(8,128)S(1)}, f32[896,768]{1,0:T(8,128)}, u32[]{:S(2)}) copy-start(f32[896,768]{1,0:T(8,128)} %fusion.2) | copy-start | bytes 8257540
  64.3 1.2 %copy-start.9 = (bf16[64,448]{1,0:T(8,128)(2,1)S(1)}, bf16[64,448]{1,0:T(8,128)(2,1)}, u32[]{:S(2)}) copy-start(bf16[64,448]{1,0:T(8,128)(2,1)} %get-tuple-element.51) | copy-start | bytes 172036
  65.5 1.0 %copy-start.5 = (bf16[384,384]{1,0:T(8,128)(2,1)S(1)}, bf16[384,384]{1,0:T(8,128)(2,1)}, u32[]{:S(2)}) copy-start(bf16[384,384]{1,0:T(8,128)(2,1)} %get-tuple-element.38) | copy-start | bytes 884740
  65.5 1.0 %copy-start.7 = (bf16[384,384]{1,0:T(8,128)(2,1)S(1)}, bf16[384,384]{1,0:T(8,128)(2,1)}, u32[]{:S(2)}) copy-start(bf16[384,384]{1,0:T(8,128)(2,1)} %get-tuple-element.39) | copy-start | bytes 884740
  65.8 1.6 %copy-start.4 = (bf16[384,384]{1,0:T(8,128)(2,1)S(1)}, bf16[384,384]{1,0:T(8,128)(2,1)}, u32[]{:S(2)}) copy-start(bf16[384,384]{1,0:T(8,128)(2,1)} %copy-done.3) | copy-start | bytes 884740
  67.4 7.2 %collective-permute-start.3 = (bf16[384,384]{1,0:T(8,128)(2,1)S(1)}, bf16[384,384]{1,0:T(8,128)(2,1)}, u32[]{:S(2)}, u32[]{:S(2)}) collective-permute-start(bf16[384,384]{1,0:T(8,128)(2,1)S(1)} %copy-done.4), channel_id=1, source_target_pairs={{0,28},{4,0},{8,4},{12,8},{16,12},{20,16},{24,20},{28,24},{1,29},{... | collective-permute-start | bytes 884744 | tf_op jit(solution)/shard_map/ppermute | solution.py:34
  80.9 1.0 %copy-start.1 = (bf16[448,384]{1,0:T(8,128)(2,1)S(1)}, bf16[448,384]{1,0:T(8,128)(2,1)}, u32[]{:S(2)}) copy-start(bf16[448,384]{1,0:T(8,128)(2,1)} %get-tuple-element.5) | copy-start | bytes 1032196
  81.2 1.0 %copy-start.6 = (bf16[384,384]{1,0:T(8,128)(2,1)S(1)}, bf16[384,384]{1,0:T(8,128)(2,1)}, u32[]{:S(2)}) copy-start(bf16[384,384]{1,0:T(8,128)(2,1)} %get-tuple-element.38) | copy-start | bytes 884740
  81.2 1.1 %copy-start.8 = (bf16[384,384]{1,0:T(8,128)(2,1)S(1)}, bf16[384,384]{1,0:T(8,128)(2,1)}, u32[]{:S(2)}) copy-start(bf16[384,384]{1,0:T(8,128)(2,1)} %get-tuple-element.39) | copy-start | bytes 884740
  81.9 0.9 %copy-start.10 = (f32[64,384]{1,0:T(8,128)S(1)}, f32[64,384]{1,0:T(8,128)}, u32[]{:S(2)}) copy-start(f32[64,384]{1,0:T(8,128)} %fusion.116) | copy-start | bytes 294916
where the time goes:
time: 84.5 us; the launch traced here: 84 us
  other arithmetic  33.2 us (39%)
  matrix products  22.4 us (27%)
  waiting for transfers between devices  13.5 us (16%)
  between operations  6.23 us (7%)
  starting transfers between devices  5.24 us (6%)
  local copies, waits for them, and re-layouts  3.51 us (4%)
    dot_general x9, matrix products, complex_left(): product = jnp.dot(stacked, values, preferred_element_type=jnp.float32)  19.8 us
    ppermute x6, waiting for transfers between devices, passed_along(): lax.ppermute(array, axis, [(i, (i + by) % count) for i in range(count)])  13.5 us
    convert_element_type x3, other arithmetic, trig_pair(): jnp.sin(angles).astype(jnp.bfloat16)  9.07 us
    another operation x8, other arithmetic  6.78 us
    neg x1, other arithmetic, forward_columns(): return jnp.concatenate([cosine, -sine_part], axis=1)  4.65 us
    convert_element_type x1, other arithmetic, trig_pair(): jnp.cos(angles).astype(jnp.bfloat16)  4.58 us
    mul x1, other arithmetic, inverse_columns(): return jnp.concatenate([cosine * weights, -sine_part * weights], axis=0)  3.32 us
    ppermute x1, starting transfers between devices, from_behind(): return lax.ppermute(array, axis, pairs)  2.83 us
  transfers between devices with their start and end apart: 7, of which 3 were waited for; matrix products, arithmetic and copies ran while one was open for 48% of the time, Pallas kernels for 0%

commit v1 on v0

v1 whole, which is shorter than its diff:
```python
import math

import jax
import jax.numpy as jnp
import ml_dtypes
import numpy as np
from jax import lax
from jax.experimental import pallas as pl
from jax.experimental.pallas import tpu as pltpu
from jax.sharding import PartitionSpec as P

TS = 384
TC = 384
MH = 64
STEPS = 4
NANG = 360
MR = 447
LR = 448
LC = 768
HALF = 384
PAIRS = LR // 2
EDGE = 16
ROWS = LR + EDGE

AMPLITUDE = 0.07
WAVELENGTH = 0.0197
BASE_DEFOCUS = 8000.0
DEFOCUS_STEP = 1000.0

HBM = pl.BlockSpec(memory_space=pltpu.HBM)
SMEM = pl.BlockSpec(memory_space=pltpu.SMEM)
VMEM = pl.BlockSpec(memory_space=pltpu.VMEM)


def trig_pair(left_count, right_count, length):
    ids = np.arange(left_count)[:, None] * np.arange(right_count)[None, :] % length
    angles = ids.astype(np.float32) * np.float32(2.0 * math.pi / length)
    return np.cos(angles), np.sin(angles)


def paired_rows():
    cosine, sine = trig_pair(PAIRS + 1, LR, LR)
    zeros = np.zeros((EDGE - 1, LR), np.float32)
    rows = np.concatenate([cosine[:PAIRS], sine[:PAIRS], cosine[PAIRS:], zeros], axis=0)
    return rows.astype(ml_dtypes.bfloat16)


def forward_columns():
    cosine, sine = trig_pair(TC, HALF, LC)
    return np.concatenate([cosine, sine], axis=1).astype(ml_dtypes.bfloat16)


def inverse_columns():
    cosine, sine = trig_pair(HALF, TC, LC)
    weights = np.where(np.arange(HALF) == 0, 1.0, 2.0).astype(np.float32)[:, None]
    cosine = cosine.astype(ml_dtypes.bfloat16).astype(np.float32) * weights
    sine = sine.astype(ml_dtypes.bfloat16).astype(np.float32) * weights
    return np.concatenate([cosine, -sine], axis=0).astype(ml_dtypes.bfloat16)


def dot(left, right):
    return jnp.dot(left, right, preferred_element_type=jnp.float32)


def spectrum_of(template, rows, cols):
    half_way = dot(rows[:, :TS], template[...]).astype(jnp.bfloat16)
    return dot(half_way, cols[...]).astype(jnp.bfloat16)


def angle_rows(orient_id):
    turns = jnp.broadcast_to(orient_id[...], (EDGE // 2, HALF)).astype(jnp.float32) * (2.0 * math.pi / NANG)
    return jnp.concatenate([jnp.cos(turns), jnp.sin(turns)], axis=0).astype(jnp.bfloat16)


def first_kernel(
    bins,
    strip_far,
    template_far,
    rows_far,
    cols_far,
    rows,
    cols,
    own_part,
    ctf,
    spectrum,
    strip,
    template,
    arrived,
):
    pairs = (
        (rows_far, rows),
        (cols_far, cols),
        (template_far, template),
        (strip_far, strip),
    )
    copies = [
        pltpu.make_async_copy(source, target, arrived.at[i])
        for i, (source, target) in enumerate(pairs)
    ]
    for copy in copies:
        copy.start()
    shape = ctf.shape
    row_ids = lax.broadcasted_iota(jnp.int32, shape, 0)
    col_ids = lax.broadcasted_iota(jnp.int32, shape, 1)
    freq_rows = row_ids.astype(jnp.float32) / LR
    freq_cols = col_ids.astype(jnp.float32) / LC
    radius = freq_rows * freq_rows + freq_cols * freq_cols
    defocus = BASE_DEFOCUS + DEFOCUS_STEP * bins[0].astype(jnp.float32)
    phases = math.pi * WAVELENGTH * defocus * radius
    values = -(
        math.sqrt(1.0 - AMPLITUDE * AMPLITUDE) * jnp.sin(phases) + AMPLITUDE * jnp.cos(phases)
    )
    ctf[...] = values * jnp.where(row_ids == 0, 0.5, 1.0)
    for copy in copies:
        copy.wait()
    spectrum[...] = spectrum_of(template, rows, cols)
    half_way = dot(rows[:, :MR], strip[...]).astype(jnp.bfloat16)
    own_part[...] = dot(half_way, cols[...])


def far_kernel(far, rows, cols, far_id, far_packed):
    far_packed[:ROWS, :] = spectrum_of(far, rows, cols)
    turn = angle_rows(far_id)
    far_packed[ROWS:, :] = jnp.concatenate([turn, turn], axis=1)


def near_kernel(near, rows, cols, near_spectrum):
    near_spectrum[...] = spectrum_of(near, rows, cols)


def blocks(values):
    upper, lower, edge = values[:PAIRS], values[PAIRS:LR], values[LR:ROWS]
    return tuple(
        block.astype(jnp.float32)
        for part in (upper, lower, edge)
        for block in (part[:, :HALF], part[:, HALF:])
    )


def multiply(micro, spectrum, product):
    for row in range(0, PAIRS, EDGE):
        up, down = slice(row, row + EDGE), slice(PAIRS + row, PAIRS + row + EDGE)
        for col in range(0, HALF, 128):
            real, imag = slice(col, col + 128), slice(HALF + col, HALF + col + 128)
            t_a, t_b, t_d, t_e = (
                spectrum[place].astype(jnp.float32)
                for place in ((up, real), (up, imag), (down, real), (down, imag))
            )
            up_real, up_imag = micro[up, real], micro[up, imag]
            down_real, down_imag = micro[down, real], micro[down, imag]
            s_real, s_imag = t_a - t_e, t_b + t_d
            r_real, r_imag = t_a + t_e, t_b - t_d
            p_real = up_real * s_real - up_imag * s_imag
            p_imag = up_real * s_imag + up_imag * s_real
            q_real = down_real * r_real - down_imag * r_imag
            q_imag = down_real * r_imag + down_imag * r_real
            product[up, real] = (p_real + q_real).astype(jnp.bfloat16)
            product[up, imag] = (p_imag + q_imag).astype(jnp.bfloat16)
            product[down, real] = (q_imag - p_imag).astype(jnp.bfloat16)
            product[down, imag] = (p_real - q_real).astype(jnp.bfloat16)
    t_x = spectrum[LR:ROWS, :HALF].astype(jnp.float32)
    t_y = spectrum[LR:ROWS, HALF:].astype(jnp.float32)
    edge_real, edge_imag = micro[LR:, :HALF], micro[LR:, HALF:]
    product[LR:, :HALF] = (edge_real * t_x - edge_imag * t_y).astype(jnp.bfloat16)
    product[LR:, HALF:] = (edge_real * t_y + edge_imag * t_x).astype(jnp.bfloat16)


def third_kernel(
    halo,
    own_part,
    ctf,
    rows,
    cols,
    rows_back,
    own_spectrum,
    far_spectrum,
    near_spectrum,
    micro,
    back_early,
    products,
):
    half_way = dot(rows[:, :MR], halo[...])
    lanes = lax.broadcasted_iota(jnp.int32, half_way.shape, 1)
    half_way = jnp.where(lanes < TC - 1, half_way, 0.0).astype(jnp.bfloat16)
    lanes = lax.broadcasted_iota(jnp.int32, (1, 2 * HALF), 1)
    signs = jnp.where(lanes % 2 == 0, 1.0, -1.0)
    m_a, m_b, m_d, m_e, m_x, m_y = blocks(own_part[...] + signs * dot(half_way, cols[...]))
    ctf_rows, ctf_edge = ctf[:PAIRS, :], ctf[PAIRS:, :]
    micro[:PAIRS, :HALF] = ctf_rows * (m_a - m_e)
    micro[:PAIRS, HALF:] = -(ctf_rows * (m_b + m_d))
    micro[PAIRS:LR, :HALF] = ctf_rows * (m_a + m_e)
    micro[PAIRS:LR, HALF:] = ctf_rows * (m_d - m_b)
    micro[LR:, :HALF] = ctf_edge * m_x
    micro[LR:, HALF:] = -(ctf_edge * m_y)
    for step, spectrum in enumerate((own_spectrum, far_spectrum, near_spectrum)):
        product = products.at[step]
        multiply(micro, spectrum, product)
        back_early[step * MH : (step + 1) * MH, :] = dot(rows_back[...], product[...]).astype(
            jnp.bfloat16
        )


def last_kernel(
    micro,
    back_early,
    late_packed,
    own_id,
    near_id,
    far_packed,
    rows_back,
    cols_back,
    peak,
    total,
    squares,
    orient_cos,
    orient_sin,
    product,
):
    multiply(micro, late_packed, product)
    back_late = dot(rows_back[...], product[...]).astype(jnp.bfloat16)
    scale = 1.0 / (TS * LR * LC)
    corr_early = dot(back_early[...], cols_back[...]) * scale
    corr_late = dot(back_late, cols_back[...]) * scale
    corrs = [corr_early[step * MH : (step + 1) * MH, :] for step in range(STEPS - 1)] + [corr_late]
    turns = (
        angle_rows(own_id),
        far_packed[ROWS:, :HALF],
        angle_rows(near_id),
        late_packed[ROWS:, :HALF],
    )
    sums = None
    for corr, turn in zip(corrs, turns):
        doubled = 2.0 * corr
        weight = jnp.maximum(doubled, 0.0) + jnp.log1p(jnp.exp(-jnp.abs(doubled)))
        cosine, sine = turn[0:1].astype(jnp.float32), turn[8:9].astype(jnp.float32)
        fresh = (corr, corr, corr * corr, weight, weight * cosine, weight * sine)
        if sums is None:
            sums = fresh
        else:
            sums = (jnp.maximum(sums[0], fresh[0]),) + tuple(
                old + new for old, new in zip(sums[1:], fresh[1:])
            )
    peak[...] = sums[0]
    total[...] = sums[1]
    squares[...] = sums[2]
    orient_cos[...] = sums[4] / sums[3]
    orient_sin[...] = sums[5] / sums[3]


def along(array, sources):
    return lax.ppermute(array, "mic", [(source, place) for place, source in enumerate(sources)])


def call(kernel, name, flops, out_shape, in_specs, scratch_shapes=()):
    return pl.pallas_call(
        kernel,
        out_shape=out_shape,
        in_specs=in_specs,
        out_specs=jax.tree.map(lambda _: VMEM, out_shape),
        scratch_shapes=scratch_shapes,
        compiler_params=pltpu.CompilerParams(vmem_limit_bytes=24 * 1024 * 1024),
        cost_estimate=pl.CostEstimate(flops=flops, bytes_accessed=10**3, transcendentals=0),
        name=name,
    )


def body(micrograph, templates, orient_ids, defocus_bins):
    rows_far = jnp.asarray(paired_rows())
    cols_far = jnp.asarray(forward_columns())
    rows_back = jnp.asarray(np.ascontiguousarray(paired_rows()[:, :MH].T))
    cols_back = jnp.asarray(inverse_columns())
    count = lax.axis_size("mic")
    tiles = lax.axis_size("tile")
    strip = micrograph[0]
    own = templates[0]
    near_places = [(d + (1 if d % 2 == 0 else 3)) % count for d in range(count)]
    far_places = [(d + 2) % count for d in range(count)]

    halo = lax.ppermute(strip, "tile", [(i + 1, i) for i in range(tiles - 1)])
    far = along(own, far_places)
    near = along(own, near_places)
    own_id = orient_ids.reshape(1, 1)
    near_id, far_id = along(own_id, near_places), along(own_id, far_places)

    bf16, f32 = jnp.bfloat16, jnp.float32
    spectrum_type = jax.ShapeDtypeStruct((ROWS, 2 * HALF), bf16)
    own_inputs = [
        pltpu.with_memory_space_constraint(x, pltpu.HBM) for x in (strip, own, rows_far, cols_far)
    ]
    rows, cols, own_part, ctf, own_spectrum = call(
        first_kernel,
        "own_spectra",
        10**9,
        (
            jax.ShapeDtypeStruct(rows_far.shape, bf16),
            jax.ShapeDtypeStruct(cols_far.shape, bf16),
            jax.ShapeDtypeStruct((ROWS, 2 * HALF), f32),
            jax.ShapeDtypeStruct((PAIRS + EDGE, HALF), f32),
            spectrum_type,
        ),
        [SMEM] + [HBM] * 4,
        [
            pltpu.VMEM((MR, TC), bf16),
            pltpu.VMEM((TS, TS), bf16),
            pltpu.SemaphoreType.DMA((4,)),
        ],
    )(defocus_bins, *own_inputs)
    far, halo, own_spectrum = lax.optimization_barrier((far, halo, own_spectrum))
    far_packed = call(
        far_kernel,
        "far_spectrum",
        10**5,
        jax.ShapeDtypeStruct((ROWS + EDGE, 2 * HALF), bf16),
        [VMEM] * 4,
    )(far, rows, cols, far_id)
    late_packed = along(far_packed, [d ^ 1 for d in range(count)])
    near_spectrum = call(near_kernel, "near_spectrum", 10**10, spectrum_type, [VMEM] * 3)(
        near, rows, cols
    )
    micro, back_early = call(
        third_kernel,
        "strip_spectrum",
        10**9,
        (
            jax.ShapeDtypeStruct((ROWS, 2 * HALF), f32),
            jax.ShapeDtypeStruct(((STEPS - 1) * MH, 2 * HALF), bf16),
        ),
        [VMEM] * 9,
        [pltpu.VMEM((STEPS - 1, ROWS, 2 * HALF), bf16)],
    )(halo, own_part, ctf, rows, cols, rows_back, own_spectrum, far_packed, near_spectrum)
    results = call(
        last_kernel,
        "match",
        10**5,
        (jax.ShapeDtypeStruct((MH, TC), f32),) * 5,
        [VMEM] * 8,
        [pltpu.VMEM((ROWS, 2 * HALF), bf16)],
    )(micro, back_early, late_packed, own_id, near_id, far_packed, rows_back, cols_back)
    return tuple(result[None] for result in results)


def solution(mesh):
    tiled = P("mic", None, "tile")
    return jax.shard_map(
        body,
        mesh=mesh,
        in_specs=(tiled, P("mic", None, None), P("mic"), P("mic")),
        out_specs=(tiled,) * 5,
        check_vma=False,
    )
```

time: 84.5 us -> 22.3 us (0.26)
  other arithmetic: 33.2 us -> 0 us
  matrix products: 22.4 us -> 0 us
  waiting for transfers between devices: 13.5 us -> 1.21 us
  Pallas kernels: 0 us -> 10.7 us
  between operations: 6.23 us -> 2.02 us
  local copies, waits for them, and re-layouts: 3.51 us -> 0.01 us
  starting transfers between devices: 5.24 us -> 8.16 us
    dot_general x13 -> x0, matrix products: 22.4 us -> none  [the longest x9 19.8 us: complex_left(): product = jnp.dot(stacked, values, preferred_element_type=jnp.float32)]
    convert_element_type x6 -> x0, other arithmetic: 13.8 us -> none  [the longest x3 9.07 us: trig_pair(): jnp.sin(angles).astype(jnp.bfloat16)]
    ppermute x7 -> x6, waiting for transfers between devices: 13.5 us -> 1.21 us  [the longest x5 1.21 us: along(): lax.ppermute(array, 'mic', [(source, place) for place, source in enumerat...]
    pallas_call x0 -> x5, Pallas kernels: none -> 10.7 us  [the longest x1 2.94 us: body(): call(first_kernel, 'own_spectra', 10 ** 9, (jax.ShapeDtypeStruct(rows_far...]
    neg x2 -> x0, other arithmetic: 7.23 us -> none  [the longest x1 4.65 us: forward_columns(): return jnp.concatenate([cosine, -sine_part], axis=1)]
    another operation x9 -> x0, other arithmetic: 6.86 us -> none
    mul x3 -> x0, other arithmetic: 3.34 us -> none  [the longest x1 3.32 us: inverse_columns(): return jnp.concatenate([cosine * weights, -sine_part * weights], axis=0)]
    ppermute x7 -> x6, starting transfers between devices: 5.24 us -> 8.16 us  [the longest x5 6.06 us: along(): lax.ppermute(array, 'mic', [(source, place) for place, source in enumerat...]
  transfers between devices with their start and end apart: 7 -> 6, of which waited for: 3 -> 2; matrix products, arithmetic and copies ran while one was open for 48% -> 0% of each run, Pallas kernels for 0% -> 37%
where the time goes in v1:
time: 22.3 us; the launch traced here: 22.1 us
  Pallas kernels  10.7 us (48%)
  starting transfers between devices  8.16 us (37%)
  between operations  2.02 us (9%)
  waiting for transfers between devices  1.21 us (5%)
    ppermute x5, starting transfers between devices, along(): lax.ppermute(array, 'mic', [(source, place) for place, source in enumerat...  6.06 us
    pallas_call x1, Pallas kernels, body(): call(first_kernel, 'own_spectra', 10 ** 9, (jax.ShapeDtypeStruct(rows_far...  2.94 us
    pallas_call x1, Pallas kernels, body(): call(third_kernel, 'strip_spectrum', 10 ** 9, (jax.ShapeDtypeStruct((ROWS...  2.79 us
    pallas_call x1, Pallas kernels, body(): call(last_kernel, 'match', 10 ** 5, (jax.ShapeDtypeStruct((MH, TC), f32),...  2.52 us
    ppermute x1, starting transfers between devices, body(): halo = lax.ppermute(strip, 'tile', [(i + 1, i) for i in range(tiles - 1)])  2.09 us
    pallas_call x1, Pallas kernels, body(): call(far_kernel, 'far_spectrum', 10 ** 5, jax.ShapeDtypeStruct((ROWS + ED...  1.53 us
    ppermute x5, waiting for transfers between devices, along(): lax.ppermute(array, 'mic', [(source, place) for place, source in enumerat...  1.21 us
    pallas_call x1, Pallas kernels, body(): call(near_kernel, 'near_spectrum', 10 ** 10, spectrum_type, [VMEM] * 3)  0.89 us
  transfers between devices with their start and end apart: 6, of which 2 were waited for; matrix products, arithmetic and copies ran while one was open for 0% of the time, Pallas kernels for 37%

profile of v1, /device:TPU:27, one launch (start us, length us, event | category | flops | bytes accessed | tf_op | source)
XLA Modules:
  0.0 22.1 jit_solution(7060338577663433321)
XLA Ops:
  0.6 2.1 %collective-permute-start.1 = (bf16[447,384]{1,0:T(8,128)(2,1)}, bf16[447,384]{1,0:T(8,128)(2,1)S(1)}, u32[]{:S(2)}, u32[]{:S(2)}) collective-permute-start(bf16[447,384]{1,0:T(8,128)(2,1)} %bitcast.9), channel_id=1, source_target_pairs={{1,0},{2,1},{3,2},{5,4},{6,5},{7,6},{9,8},{10,9},{11,10},{13,12},{... | collective-permute-start | bytes 1029896 | tf_op jit(solution)/shard_map/ppermute | solution.py:279
  2.7 0.3 %collective-permute-start = (bf16[384,384]{1,0:T(8,128)(2,1)}, bf16[384,384]{1,0:T(8,128)(2,1)S(1)}, u32[]{:S(2)}, u32[]{:S(2)}) collective-permute-start(bf16[384,384]{1,0:T(8,128)(2,1)} %bitcast.11), channel_id=1, source_target_pairs={{8,0},{12,4},{16,8},{20,12},{24,16},{28,20},{0,24},{4,28},{9,1},{1... | collective-permute-start | bytes 884744 | tf_op jit(solution)/shard_map/ppermute | solution.py:251
  3.0 1.2 %collective-permute-start.3 = (bf16[384,384]{1,0:T(8,128)(2,1)}, bf16[384,384]{1,0:T(8,128)(2,1)S(1)}, u32[]{:S(2)}, u32[]{:S(2)}) collective-permute-start(bf16[384,384]{1,0:T(8,128)(2,1)} %bitcast.12), channel_id=1, source_target_pairs={{4,0},{16,4},{12,8},{24,12},{20,16},{0,20},{28,24},{8,28},{5,1},{1... | collective-permute-start | bytes 884744 | tf_op jit(solution)/shard_map/ppermute | solution.py:251
  4.3 2.2 %collective-permute-start.2 = (s32[1,1]{1,0:T(1,128)}, s32[1,1]{1,0:T(1,128)}, u32[]{:S(2)}, u32[]{:S(2)}) collective-permute-start(s32[1,1]{1,0:T(1,128)} %bitcast.2), channel_id=1, source_target_pairs={{8,0},{12,4},{16,8},{20,12},{24,16},{28,20},{0,24},{4,28},{9,1},{1... | collective-permute-start | bytes 20 | tf_op jit(solution)/shard_map/ppermute | solution.py:251
  6.4 0.3 %collective-permute-start.5 = (s32[1,1]{1,0:T(1,128)}, s32[1,1]{1,0:T(1,128)}, u32[]{:S(2)}, u32[]{:S(2)}) collective-permute-start(s32[1,1]{1,0:T(1,128)} %bitcast.2), channel_id=1, source_target_pairs={{4,0},{16,4},{12,8},{24,12},{20,16},{0,20},{28,24},{8,28},{5,1},{1... | collective-permute-start | bytes 20 | tf_op jit(solution)/shard_map/ppermute | solution.py:251
  8.0 2.9 %own_spectra.1 = (bf16[464,448]{1,0:T(8,128)(2,1)S(1)}, bf16[384,768]{1,0:T(8,128)(2,1)S(1)}, f32[464,768]{1,0:T(8,128)S(1)}, f32[240,384]{1,0:T(8,128)S(1)}, bf16[464,768]{1,0:T(8,128)(2,1)S(1)}) custom-call(s32[1]{0:T(128)S(6)} %copy.14.bins, bf16[447,384]{1,0:T(8,128)(2,1)} %bitcast.10, bf16[384,384]{1,0:T(8,128)(2,1)} %bitcast.13, ...), custom_call_target="tpu_custom_call" | custom-call | flops 1000000000 | bytes 1000 | tf_op jit(solution)/shard_map/own_spectra/pallas_call | solution.py:290
  11.0 0.5 %collective-permute-done.far = bf16[384,384]{1,0:T(8,128)(2,1)S(1)} collective-permute-done((bf16[384,384]{1,0:T(8,128)(2,1)}, bf16[384,384]{1,0:T(8,128)(2,1)S(1)}, u32[]{:S(2)}, u32[]{:S(2)}) %collective-permute-start) | collective-permute-done | bytes 294944 | tf_op jit(solution)/shard_map/ppermute | solution.py:251
  11.5 0.0 collective-permute-done.1.halo
  11.5 0.0 collective-permute-done.2.far_id
  11.5 1.5 %far_spectrum.1.far_packed = bf16[480,768]{1,0:T(8,128)(2,1)S(1)} custom-call(bf16[384,384]{1,0:T(8,128)(2,1)S(1)} %collective-permute-done.far, bf16[464,448]{1,0:T(8,128)(2,1)S(1)} %get-tuple-element.24.rows, bf16[384,768]{1,0:T(8,128)(2,1)S(1)} %get-tuple-element.25.cols, s32[1,1]{1,0:T(1,128)} %collective-permute-done.2.far_id), custom_call_target="tpu_custom_call" | custom-call | flops 100000 | bytes 1000 | tf_op jit(solution)/shard_map/far_spectrum/pallas_call | solution.py:309
  13.0 0.0 copy-start.1
  13.1 2.1 %collective-permute-start.4 = (bf16[480,768]{1,0:T(8,128)(2,1)S(1)}, bf16[480,768]{1,0:T(8,128)(2,1)S(1)}, u32[]{:S(2)}, u32[]{:S(2)}) collective-permute-start(bf16[480,768]{1,0:T(8,128)(2,1)S(1)} %far_spectrum.1.far_packed), channel_id=1, source_target_pairs={{4,0},{0,4},{12,8},{8,12},{20,16},{16,20},{28,24},{24,28},{5,1},{1... | collective-permute-start | bytes 2211848 | tf_op jit(solution)/shard_map/ppermute | solution.py:251
  15.1 0.7 %collective-permute-done.3.near = bf16[384,384]{1,0:T(8,128)(2,1)S(1)} collective-permute-done((bf16[384,384]{1,0:T(8,128)(2,1)}, bf16[384,384]{1,0:T(8,128)(2,1)S(1)}, u32[]{:S(2)}, u32[]{:S(2)}) %collective-permute-start.3) | collective-permute-done | bytes 294944 | tf_op jit(solution)/shard_map/ppermute | solution.py:251
  15.8 0.9 %near_spectrum.1 = bf16[464,768]{1,0:T(8,128)(2,1)S(1)} custom-call(bf16[384,384]{1,0:T(8,128)(2,1)S(1)} %collective-permute-done.3.near, bf16[464,448]{1,0:T(8,128)(2,1)S(1)} %get-tuple-element.24.rows, bf16[384,768]{1,0:T(8,128)(2,1)S(1)} %get-tuple-element.25.cols), custom_call_target="tpu_custom_call" | custom-call | flops 10000000000 | bytes 1000 | tf_op jit(solution)/shard_map/near_spectrum/pallas_call | solution.py:317
  16.7 0.0 copy-done.1
  16.7 0.0 copy-start
  16.7 2.8 %strip_spectrum.1 = (f32[464,768]{1,0:T(8,128)S(1)}, bf16[192,768]{1,0:T(8,128)(2,1)S(1)}) custom-call(bf16[447,384]{1,0:T(8,128)(2,1)S(1)} %collective-permute-done.1.halo, f32[464,768]{1,0:T(8,128)S(1)} %get-tuple-element.22.own_part, f32[240,384]{1,0:T(8,128)S(1)} %get-tuple-element.23.ctf, bf16[464,448]{1,0:T(8,128)(2,1)S(1)} %get-tuple-element.24.rows, ...), custom_call_target="tpu_custom_call" | custom-call | flops 1000000000 | bytes 1000 | tf_op jit(solution)/shard_map/strip_spectrum/pallas_call | solution.py:320
  19.5 0.0 collective-permute-done.5.near_id
  19.5 0.0 collective-permute-done.4.late_packed
  19.5 0.0 copy-done
  19.5 2.5 %match.1 = (f32[64,384]{1,0:T(8,128)}, f32[64,384]{1,0:T(8,128)}, f32[64,384]{1,0:T(8,128)}, f32[64,384]{1,0:T(8,128)}, f32[64,384]{1,0:T(8,128)}) custom-call(f32[464,768]{1,0:T(8,128)S(1)} %get-tuple-element.28.micro, bf16[192,768]{1,0:T(8,128)(2,1)S(1)} %get-tuple-element.29.back_early, bf16[480,768]{1,0:T(8,128)(2,1)S(1)} %collective-permute-done.4.late_packed, ...), custom_call_target="tpu_custom_call" | custom-call | flops 100000 | bytes 1000 | tf_op jit(solution)/shard_map/match/pallas_call | solution.py:331
Async XLA Ops:
  0.6 10.9 %collective-permute-start.1 = (bf16[447,384]{1,0:T(8,128)(2,1)}, bf16[447,384]{1,0:T(8,128)(2,1)S(1)}, u32[]{:S(2)}, u32[]{:S(2)}) collective-permute-start(bf16[447,384]{1,0:T(8,128)(2,1)} %bitcast.9), channel_id=1, source_target_pairs={{1,0},{2,1},{3,2},{5,4},{6,5},{7,6},{9,8},{10,9},{11,10},{13,12},{... | collective-permute-start | bytes 1029896 | tf_op jit(solution)/shard_map/ppermute | solution.py:279
  2.7 8.8 %collective-permute-start = (bf16[384,384]{1,0:T(8,128)(2,1)}, bf16[384,384]{1,0:T(8,128)(2,1)S(1)}, u32[]{:S(2)}, u32[]{:S(2)}) collective-permute-start(bf16[384,384]{1,0:T(8,128)(2,1)} %bitcast.11), channel_id=1, source_target_pairs={{8,0},{12,4},{16,8},{20,12},{24,16},{28,20},{0,24},{4,28},{9,1},{1... | collective-permute-start | bytes 884744 | tf_op jit(solution)/shard_map/ppermute | solution.py:251
  3.0 12.8 %collective-permute-start.3 = (bf16[384,384]{1,0:T(8,128)(2,1)}, bf16[384,384]{1,0:T(8,128)(2,1)S(1)}, u32[]{:S(2)}, u32[]{:S(2)}) collective-permute-start(bf16[384,384]{1,0:T(8,128)(2,1)} %bitcast.12), channel_id=1, source_target_pairs={{4,0},{16,4},{12,8},{24,12},{20,16},{0,20},{28,24},{8,28},{5,1},{1... | collective-permute-start | bytes 884744 | tf_op jit(solution)/shard_map/ppermute | solution.py:251
  4.3 7.2 %collective-permute-start.2 = (s32[1,1]{1,0:T(1,128)}, s32[1,1]{1,0:T(1,128)}, u32[]{:S(2)}, u32[]{:S(2)}) collective-permute-start(s32[1,1]{1,0:T(1,128)} %bitcast.2), channel_id=1, source_target_pairs={{8,0},{12,4},{16,8},{20,12},{24,16},{28,20},{0,24},{4,28},{9,1},{1... | collective-permute-start | bytes 20 | tf_op jit(solution)/shard_map/ppermute | solution.py:251
  6.4 13.1 %collective-permute-start.5 = (s32[1,1]{1,0:T(1,128)}, s32[1,1]{1,0:T(1,128)}, u32[]{:S(2)}, u32[]{:S(2)}) collective-permute-start(s32[1,1]{1,0:T(1,128)} %bitcast.2), channel_id=1, source_target_pairs={{4,0},{16,4},{12,8},{24,12},{20,16},{0,20},{28,24},{8,28},{5,1},{1... | collective-permute-start | bytes 20 | tf_op jit(solution)/shard_map/ppermute | solution.py:251
  13.0 3.7 %copy-start.1 = (bf16[64,464]{1,0:T(8,128)(2,1)S(1)}, bf16[64,464]{1,0:T(8,128)(2,1)}, u32[]{:S(2)}) copy-start(bf16[64,464]{1,0:T(8,128)(2,1)} %constant.10.clone.rows_back) | copy-start | bytes 178180
  13.1 6.5 %collective-permute-start.4 = (bf16[480,768]{1,0:T(8,128)(2,1)S(1)}, bf16[480,768]{1,0:T(8,128)(2,1)S(1)}, u32[]{:S(2)}, u32[]{:S(2)}) collective-permute-start(bf16[480,768]{1,0:T(8,128)(2,1)S(1)} %far_spectrum.1.far_packed), channel_id=1, source_target_pairs={{4,0},{0,4},{12,8},{8,12},{20,16},{16,20},{28,24},{24,28},{5,1},{1... | collective-permute-start | bytes 2211848 | tf_op jit(solution)/shard_map/ppermute | solution.py:251
  16.7 2.8 %copy-start = (bf16[768,384]{1,0:T(8,128)(2,1)S(1)}, bf16[768,384]{1,0:T(8,128)(2,1)}, u32[]{:S(2)}) copy-start(bf16[768,384]{1,0:T(8,128)(2,1)} %constant.11.clone.cols_back) | copy-start | bytes 1769476

commit v2 on v1

--- a/solution.py
+++ b/solution.py
@@ -27,6 +27,8 @@
 BASE_DEFOCUS = 8000.0
 DEFOCUS_STEP = 1000.0
 
+COST = (10**5, 10**5, 10**5, 10**10, 10**5)
+
 HBM = pl.BlockSpec(memory_space=pltpu.HBM)
 SMEM = pl.BlockSpec(memory_space=pltpu.SMEM)
 VMEM = pl.BlockSpec(memory_space=pltpu.VMEM)
@@ -67,9 +69,9 @@
     return dot(half_way, cols[...]).astype(jnp.bfloat16)
 
 
-def angle_rows(orient_id):
-    turns = jnp.broadcast_to(orient_id[...], (EDGE // 2, HALF)).astype(jnp.float32) * (2.0 * math.pi / NANG)
-    return jnp.concatenate([jnp.cos(turns), jnp.sin(turns)], axis=0).astype(jnp.bfloat16)
+def turn_kernel(orient_id, turn):
+    turns = jnp.full((EDGE // 2, HALF), orient_id[0]).astype(jnp.float32) * (2.0 * math.pi / NANG)
+    turn[...] = jnp.concatenate([jnp.cos(turns), jnp.sin(turns)], axis=0).astype(jnp.bfloat16)
 
 
 def first_kernel(
@@ -80,11 +82,11 @@
     cols_far,
     rows,
     cols,
+    template,
     own_part,
     ctf,
     spectrum,
     strip,
-    template,
     arrived,
 ):
     pairs = (
@@ -118,16 +120,6 @@
     own_part[...] = dot(half_way, cols[...])
 
 
-def far_kernel(far, rows, cols, far_id, far_packed):
-    far_packed[:ROWS, :] = spectrum_of(far, rows, cols)
-    turn = angle_rows(far_id)
-    far_packed[ROWS:, :] = jnp.concatenate([turn, turn], axis=1)
-
-
-def near_kernel(near, rows, cols, near_spectrum):
-    near_spectrum[...] = spectrum_of(near, rows, cols)
-
-
 def blocks(values):
     upper, lower, edge = values[:PAIRS], values[PAIRS:LR], values[LR:ROWS]
     return tuple(
@@ -137,7 +129,7 @@
     )
 
 
-def multiply(micro, spectrum, product):
+def multiply_back(micro, spectrum, rows_back, product, back):
     for row in range(0, PAIRS, EDGE):
         up, down = slice(row, row + EDGE), slice(PAIRS + row, PAIRS + row + EDGE)
         for col in range(0, HALF, 128):
@@ -163,28 +155,20 @@
     edge_real, edge_imag = micro[LR:, :HALF], micro[LR:, HALF:]
     product[LR:, :HALF] = (edge_real * t_x - edge_imag * t_y).astype(jnp.bfloat16)
     product[LR:, HALF:] = (edge_real * t_y + edge_imag * t_x).astype(jnp.bfloat16)
-
-
-def third_kernel(
-    halo,
-    own_part,
-    ctf,
-    rows,
-    cols,
-    rows_back,
-    own_spectrum,
-    far_spectrum,
-    near_spectrum,
-    micro,
-    back_early,
-    products,
-):
-    half_way = dot(rows[:, :MR], halo[...])
-    lanes = lax.broadcasted_iota(jnp.int32, half_way.shape, 1)
-    half_way = jnp.where(lanes < TC - 1, half_way, 0.0).astype(jnp.bfloat16)
+    back[...] = dot(rows_back[...], product[...]).astype(jnp.bfloat16)
+
+
+def second_kernel(far, halo, far_turn, own_part, ctf, rows, cols, far_packed, micro):
+    far_half = dot(rows[:, :TS], far[...]).astype(jnp.bfloat16)
+    halo_half = dot(rows[:, :MR], halo[...])
+    lanes = lax.broadcasted_iota(jnp.int32, halo_half.shape, 1)
+    halo_half = jnp.where(lanes < TC - 1, halo_half, 0.0).astype(jnp.bfloat16)
+    far_packed[:ROWS, :] = dot(far_half, cols[...]).astype(jnp.bfloat16)
+    far_packed[ROWS:, :HALF] = far_turn[...]
+    far_packed[ROWS:, HALF:] = far_turn[...]
     lanes = lax.broadcasted_iota(jnp.int32, (1, 2 * HALF), 1)
     signs = jnp.where(lanes % 2 == 0, 1.0, -1.0)
-    m_a, m_b, m_d, m_e, m_x, m_y = blocks(own_part[...] + signs * dot(half_way, cols[...]))
+    m_a, m_b, m_d, m_e, m_x, m_y = blocks(own_part[...] + signs * dot(halo_half, cols[...]))
     ctf_rows, ctf_edge = ctf[:PAIRS, :], ctf[PAIRS:, :]
     micro[:PAIRS, :HALF] = ctf_rows * (m_a - m_e)
     micro[:PAIRS, HALF:] = -(ctf_rows * (m_b + m_d))
@@ -192,20 +176,24 @@
     micro[PAIRS:LR, HALF:] = ctf_rows * (m_d - m_b)
     micro[LR:, :HALF] = ctf_edge * m_x
     micro[LR:, HALF:] = -(ctf_edge * m_y)
-    for step, spectrum in enumerate((own_spectrum, far_spectrum, near_spectrum)):
-        product = products.at[step]
-        multiply(micro, spectrum, product)
-        back_early[step * MH : (step + 1) * MH, :] = dot(rows_back[...], product[...]).astype(
-            jnp.bfloat16
-        )
+
+
+def third_kernel(
+    near, micro, own_spectrum, far_packed, rows, cols, rows_back, near_spectrum, back_early, products
+):
+    near_half = dot(rows[:, :TS], near[...]).astype(jnp.bfloat16)
+    multiply_back(micro, own_spectrum, rows_back, products.at[0], back_early.at[:MH])
+    near_spectrum[...] = dot(near_half, cols[...]).astype(jnp.bfloat16)
+    multiply_back(micro, far_packed, rows_back, products.at[1], back_early.at[MH:])
 
 
 def last_kernel(
     micro,
     back_early,
+    near_spectrum,
     late_packed,
-    own_id,
-    near_id,
+    own_turn,
+    near_turn,
     far_packed,
     rows_back,
     cols_back,
@@ -214,20 +202,15 @@
     squares,
     orient_cos,
     orient_sin,
-    product,
+    products,
+    back_late,
 ):
-    multiply(micro, late_packed, product)
-    back_late = dot(rows_back[...], product[...]).astype(jnp.bfloat16)
+    multiply_back(micro, near_spectrum, rows_back, products.at[0], back_late.at[:MH])
+    multiply_back(micro, late_packed, rows_back, products.at[1], back_late.at[MH:])
     scale = 1.0 / (TS * LR * LC)
-    corr_early = dot(back_early[...], cols_back[...]) * scale
-    corr_late = dot(back_late, cols_back[...]) * scale
-    corrs = [corr_early[step * MH : (step + 1) * MH, :] for step in range(STEPS - 1)] + [corr_late]
-    turns = (
-        angle_rows(own_id),
-        far_packed[ROWS:, :HALF],
-        angle_rows(near_id),
-        late_packed[ROWS:, :HALF],
-    )
+    halves = [dot(back[...], cols_back[...]) * scale for back in (back_early, back_late)]
+    corrs = [half[step * MH : (step + 1) * MH, :] for half in halves for step in range(2)]
+    turns = (own_turn[...], far_packed[ROWS:, :HALF], near_turn[...], late_packed[ROWS:, :HALF])
     sums = None
     for corr, turn in zip(corrs, turns):
         doubled = 2.0 * corr
@@ -278,64 +261,70 @@
 
     halo = lax.ppermute(strip, "tile", [(i + 1, i) for i in range(tiles - 1)])
     far = along(own, far_places)
-    near = along(own, near_places)
-    own_id = orient_ids.reshape(1, 1)
-    near_id, far_id = along(own_id, near_places), along(own_id, far_places)
+    own_turn = call(
+        turn_kernel, "turn", COST[0], jax.ShapeDtypeStruct((EDGE, HALF), jnp.bfloat16), [SMEM]
+    )(orient_ids)
+    near_turn, far_turn = along(own_turn, near_places), along(own_turn, far_places)
 
     bf16, f32 = jnp.bfloat16, jnp.float32
     spectrum_type = jax.ShapeDtypeStruct((ROWS, 2 * HALF), bf16)
     own_inputs = [
         pltpu.with_memory_space_constraint(x, pltpu.HBM) for x in (strip, own, rows_far, cols_far)
     ]
-    rows, cols, own_part, ctf, own_spectrum = call(
+    rows, cols, template, own_part, ctf, own_spectrum = call(
         first_kernel,
         "own_spectra",
-        10**9,
+        COST[1],
         (
             jax.ShapeDtypeStruct(rows_far.shape, bf16),
             jax.ShapeDtypeStruct(cols_far.shape, bf16),
+            jax.ShapeDtypeStruct(own.shape, bf16),
             jax.ShapeDtypeStruct((ROWS, 2 * HALF), f32),
             jax.ShapeDtypeStruct((PAIRS + EDGE, HALF), f32),
             spectrum_type,
         ),
         [SMEM] + [HBM] * 4,
-        [
-            pltpu.VMEM((MR, TC), bf16),
-            pltpu.VMEM((TS, TS), bf16),
-            pltpu.SemaphoreType.DMA((4,)),
-        ],
+        [pltpu.VMEM((MR, TC), bf16), pltpu.SemaphoreType.DMA((4,))],
     )(defocus_bins, *own_inputs)
+    near = along(own, near_places)
     far, halo, own_spectrum = lax.optimization_barrier((far, halo, own_spectrum))
-    far_packed = call(
-        far_kernel,
-        "far_spectrum",
-        10**5,
-        jax.ShapeDtypeStruct((ROWS + EDGE, 2 * HALF), bf16),
-        [VMEM] * 4,
-    )(far, rows, cols, far_id)
+    far_packed, micro = call(
+        second_kernel,
+        "far_and_strip",
+        COST[2],
+        (
+            jax.ShapeDtypeStruct((ROWS + EDGE, 2 * HALF), bf16),
+            jax.ShapeDtypeStruct((ROWS, 2 * HALF), f32),
+        ),
+        [VMEM] * 7,
+    )(far, halo, far_turn, own_part, ctf, rows, cols)
     late_packed = along(far_packed, [d ^ 1 for d in range(count)])
-    near_spectrum = call(near_kernel, "near_spectrum", 10**10, spectrum_type, [VMEM] * 3)(
-        near, rows, cols
-    )
-    micro, back_early = call(
+    near_spectrum, back_early = call(
         third_kernel,
-        "strip_spectrum",
-        10**9,
-        (
-            jax.ShapeDtypeStruct((ROWS, 2 * HALF), f32),
-            jax.ShapeDtypeStruct(((STEPS - 1) * MH, 2 * HALF), bf16),
-        ),
-        [VMEM] * 9,
-        [pltpu.VMEM((STEPS - 1, ROWS, 2 * HALF), bf16)],
-    )(halo, own_part, ctf, rows, cols, rows_back, own_spectrum, far_packed, near_spectrum)
+        "near_and_early",
+        COST[3],
+        (spectrum_type, jax.ShapeDtypeStruct((2 * MH, 2 * HALF), bf16)),
+        [VMEM] * 7,
+        [pltpu.VMEM((2, ROWS, 2 * HALF), bf16)],
+    )(near, micro, own_spectrum, far_packed, rows, cols, rows_back)
     results = call(
         last_kernel,
         "match",
-        10**5,
+        COST[4],
         (jax.ShapeDtypeStruct((MH, TC), f32),) * 5,
-        [VMEM] * 8,
-        [pltpu.VMEM((ROWS, 2 * HALF), bf16)],
-    )(micro, back_early, late_packed, own_id, near_id, far_packed, rows_back, cols_back)
+        [VMEM] * 9,
+        [pltpu.VMEM((2, ROWS, 2 * HALF), bf16), pltpu.VMEM((2 * MH, 2 * HALF), bf16)],
+    )(
+        micro,
+        back_early,
+        near_spectrum,
+        late_packed,
+        own_turn,
+        near_turn,
+        far_packed,
+        rows_back,
+        cols_back,
+    )
     return tuple(result[None] for result in results)
 
 

time: 22.3 us -> 20.1 us (0.901)
  Pallas kernels: 10.7 us -> 8.17 us
  waiting for transfers between devices: 1.21 us -> 1.51 us
    pallas_call x5, Pallas kernels: 10.7 us -> 8.17 us  [the longest x1 2.95 us: body(): call(first_kernel, 'own_spectra', COST[1], (jax.ShapeDtypeStruct(rows_far...]
    ppermute x5, waiting for transfers between devices: 1.21 us -> 1.51 us  [along(): lax.ppermute(array, 'mic', [(source, place) for place, source in enumerat...]
  transfers between devices with their start and end apart: 6 -> 6, of which waited for: 2 -> 3; matrix products, arithmetic and copies ran while one was open for 0% -> 0% of each run, Pallas kernels for 37% -> 30%
where the time goes in v2:
time: 20.1 us; the launch traced here: 19.8 us
  Pallas kernels  8.17 us (41%)
  starting transfers between devices  8.13 us (40%)
  between operations  2 us (10%)
  waiting for transfers between devices  1.51 us (8%)
    ppermute x5, starting transfers between devices, along(): lax.ppermute(array, 'mic', [(source, place) for place, source in enumerat...  6.04 us
    pallas_call x1, Pallas kernels, body(): call(first_kernel, 'own_spectra', COST[1], (jax.ShapeDtypeStruct(rows_far...  2.95 us
    pallas_call x1, Pallas kernels, body(): call(last_kernel, 'match', COST[4], (jax.ShapeDtypeStruct((MH, TC), f32),...  2.29 us
    ppermute x1, starting transfers between devices, body(): halo = lax.ppermute(strip, 'tile', [(i + 1, i) for i in range(tiles - 1)])  2.1 us
    ppermute x5, waiting for transfers between devices, along(): lax.ppermute(array, 'mic', [(source, place) for place, source in enumerat...  1.51 us
    pallas_call x1, Pallas kernels, body(): call(second_kernel, 'far_and_strip', COST[2], (jax.ShapeDtypeStruct((ROWS...  1.46 us
    pallas_call x1, Pallas kernels, body(): call(third_kernel, 'near_and_early', COST[3], (spectrum_type, jax.ShapeDt...  1.43 us
  transfers between devices with their start and end apart: 6, of which 3 were waited for; matrix products, arithmetic and copies ran while one was open for 0% of the time, Pallas kernels for 30%

profile of v2, /device:TPU:27, one launch (start us, length us, event | category | flops | bytes accessed | tf_op | source)
XLA Modules:
  0.0 19.8 jit_solution(14553875674746932388)
XLA Ops:
  0.6 2.1 %collective-permute-start.1 = (bf16[447,384]{1,0:T(8,128)(2,1)}, bf16[447,384]{1,0:T(8,128)(2,1)S(1)}, u32[]{:S(2)}, u32[]{:S(2)}) collective-permute-start(bf16[447,384]{1,0:T(8,128)(2,1)} %bitcast.7), channel_id=1, source_target_pairs={{1,0},{2,1},{3,2},{5,4},{6,5},{7,6},{9,8},{10,9},{11,10},{13,12},{... | collective-permute-start | bytes 1029896 | tf_op jit(solution)/shard_map/ppermute | solution.py:262
  2.7 0.3 %collective-permute-start = (bf16[384,384]{1,0:T(8,128)(2,1)}, bf16[384,384]{1,0:T(8,128)(2,1)S(1)}, u32[]{:S(2)}, u32[]{:S(2)}) collective-permute-start(bf16[384,384]{1,0:T(8,128)(2,1)} %bitcast.9), channel_id=1, source_target_pairs={{8,0},{12,4},{16,8},{20,12},{24,16},{28,20},{0,24},{4,28},{9,1},{1... | collective-permute-start | bytes 884744 | tf_op jit(solution)/shard_map/ppermute | solution.py:234
  3.0 1.2 %collective-permute-start.3 = (bf16[384,384]{1,0:T(8,128)(2,1)}, bf16[384,384]{1,0:T(8,128)(2,1)S(1)}, u32[]{:S(2)}, u32[]{:S(2)}) collective-permute-start(bf16[384,384]{1,0:T(8,128)(2,1)} %bitcast.10), channel_id=1, source_target_pairs={{4,0},{16,4},{12,8},{24,12},{20,16},{0,20},{28,24},{8,28},{5,1},{1... | collective-permute-start | bytes 884744 | tf_op jit(solution)/shard_map/ppermute | solution.py:234
  5.0 2.2 %collective-permute-start.2 = (bf16[16,384]{1,0:T(8,128)(2,1)S(1)}, bf16[16,384]{1,0:T(8,128)(2,1)S(1)}, u32[]{:S(2)}, u32[]{:S(2)}) collective-permute-start(bf16[16,384]{1,0:T(8,128)(2,1)S(1)} %turn.1.own_turn), channel_id=1, source_target_pairs={{8,0},{12,4},{16,8},{20,12},{24,16},{28,20},{0,24},{4,28},{9,1},{1... | collective-permute-start | bytes 36872 | tf_op jit(solution)/shard_map/ppermute | solution.py:234
  7.2 0.3 %collective-permute-start.5 = (bf16[16,384]{1,0:T(8,128)(2,1)S(1)}, bf16[16,384]{1,0:T(8,128)(2,1)S(1)}, u32[]{:S(2)}, u32[]{:S(2)}) collective-permute-start(bf16[16,384]{1,0:T(8,128)(2,1)S(1)} %turn.1.own_turn), channel_id=1, source_target_pairs={{4,0},{16,4},{12,8},{24,12},{20,16},{0,20},{28,24},{8,28},{5,1},{1... | collective-permute-start | bytes 36872 | tf_op jit(solution)/shard_map/ppermute | solution.py:234
  8.1 3.0 %own_spectra.1 = (bf16[464,448]{1,0:T(8,128)(2,1)S(1)}, bf16[384,768]{1,0:T(8,128)(2,1)S(1)}, bf16[384,384]{1,0:T(8,128)(2,1)}, f32[464,768]{1,0:T(8,128)S(1)}, ...) custom-call(s32[1]{0:T(128)S(6)} %copy.14.bins, bf16[447,384]{1,0:T(8,128)(2,1)} %bitcast.8, ...), custom_call_target="tpu_custom_call" | custom-call | flops 100000 | bytes 1000 | tf_op jit(solution)/shard_map/own_spectra/pallas_call | solution.py:274
  11.1 0.4 %collective-permute-done.far = bf16[384,384]{1,0:T(8,128)(2,1)S(1)} collective-permute-done((bf16[384,384]{1,0:T(8,128)(2,1)}, bf16[384,384]{1,0:T(8,128)(2,1)S(1)}, u32[]{:S(2)}, u32[]{:S(2)}) %collective-permute-start) | collective-permute-done | bytes 294944 | tf_op jit(solution)/shard_map/ppermute | solution.py:234
  11.5 0.0 collective-permute-done.1.halo
  11.5 0.3 %collective-permute-done.2.far_turn = bf16[16,384]{1,0:T(8,128)(2,1)S(1)} collective-permute-done((bf16[16,384]{1,0:T(8,128)(2,1)S(1)}, bf16[16,384]{1,0:T(8,128)(2,1)S(1)}, u32[]{:S(2)}, u32[]{:S(2)}) %collective-permute-start.2) | collective-permute-done | bytes 12320 | tf_op jit(solution)/shard_map/ppermute | solution.py:234
  11.8 0.0 copy-start.1
  11.8 1.5 %far_and_strip.1 = (bf16[480,768]{1,0:T(8,128)(2,1)S(1)}, f32[464,768]{1,0:T(8,128)S(1)}) custom-call(bf16[384,384]{1,0:T(8,128)(2,1)S(1)} %collective-permute-done.far, bf16[447,384]{1,0:T(8,128)(2,1)S(1)} %collective-permute-done.1.halo, bf16[16,384]{1,0:T(8,128)(2,1)S(1)} %collective-permute-done.2.far_turn, f32[464,768]{1,0:T(8,128)S(1)} %get-tuple-element.25.own_part, ...), custom_call_target="tpu_custom_call" | custom-call | flops 100000 | bytes 1000 | tf_op jit(solution)/shard_map/far_and_strip/pallas_call | solution.py:291
  13.2 2.0 %collective-permute-start.4 = (bf16[480,768]{1,0:T(8,128)(2,1)S(1)}, bf16[480,768]{1,0:T(8,128)(2,1)S(1)}, u32[]{:S(2)}, u32[]{:S(2)}) collective-permute-start(bf16[480,768]{1,0:T(8,128)(2,1)S(1)} %get-tuple-element.31.far_packed), channel_id=1, source_target_pairs={{4,0},{0,4},{12,8},{8,12},{20,16},{16,20},{28,24},{24,28},{5,1},{1... | collective-permute-start | bytes 2211848 | tf_op jit(solution)/shard_map/ppermute | solution.py:234
  15.2 0.8 %collective-permute-done.3.near = bf16[384,384]{1,0:T(8,128)(2,1)S(1)} collective-permute-done((bf16[384,384]{1,0:T(8,128)(2,1)}, bf16[384,384]{1,0:T(8,128)(2,1)S(1)}, u32[]{:S(2)}, u32[]{:S(2)}) %collective-permute-start.3) | collective-permute-done | bytes 294944 | tf_op jit(solution)/shard_map/ppermute | solution.py:234
  16.1 0.0 copy-done.1
  16.1 0.0 copy-start
  16.1 1.4 %near_and_early.1 = (bf16[464,768]{1,0:T(8,128)(2,1)S(1)}, bf16[128,768]{1,0:T(8,128)(2,1)S(1)}) custom-call(bf16[384,384]{1,0:T(8,128)(2,1)S(1)} %collective-permute-done.3.near, f32[464,768]{1,0:T(8,128)S(1)} %get-tuple-element.29.micro, bf16[464,768]{1,0:T(8,128)(2,1)S(1)} %get-tuple-element.30.own_spectrum, ...), custom_call_target="tpu_custom_call" | custom-call | flops 10000000000 | bytes 1000 | tf_op jit(solution)/shard_map/near_and_early/pallas_call | solution.py:302
  17.5 0.0 collective-permute-done.5.near_turn
  17.5 0.0 collective-permute-done.4.late_packed
  17.5 0.0 copy-done
  17.5 2.3 %match.1 = (f32[64,384]{1,0:T(8,128)}, f32[64,384]{1,0:T(8,128)}, f32[64,384]{1,0:T(8,128)}, f32[64,384]{1,0:T(8,128)}, f32[64,384]{1,0:T(8,128)}) custom-call(f32[464,768]{1,0:T(8,128)S(1)} %get-tuple-element.29.micro, bf16[128,768]{1,0:T(8,128)(2,1)S(1)} %get-tuple-element.32.back_early, bf16[464,768]{1,0:T(8,128)(2,1)S(1)} %get-tuple-element.33.near_spectrum, ...), custom_call_target="tpu_custom_call" | custom-call | flops 100000 | bytes 1000 | tf_op jit(solution)/shard_map/match/pallas_call | solution.py:310
  (1 shorter events, 0.0 us)
Async XLA Ops:
  0.6 10.9 %collective-permute-start.1 = (bf16[447,384]{1,0:T(8,128)(2,1)}, bf16[447,384]{1,0:T(8,128)(2,1)S(1)}, u32[]{:S(2)}, u32[]{:S(2)}) collective-permute-start(bf16[447,384]{1,0:T(8,128)(2,1)} %bitcast.7), channel_id=1, source_target_pairs={{1,0},{2,1},{3,2},{5,4},{6,5},{7,6},{9,8},{10,9},{11,10},{13,12},{... | collective-permute-start | bytes 1029896 | tf_op jit(solution)/shard_map/ppermute | solution.py:262
  2.7 8.8 %collective-permute-start = (bf16[384,384]{1,0:T(8,128)(2,1)}, bf16[384,384]{1,0:T(8,128)(2,1)S(1)}, u32[]{:S(2)}, u32[]{:S(2)}) collective-permute-start(bf16[384,384]{1,0:T(8,128)(2,1)} %bitcast.9), channel_id=1, source_target_pairs={{8,0},{12,4},{16,8},{20,12},{24,16},{28,20},{0,24},{4,28},{9,1},{1... | collective-permute-start | bytes 884744 | tf_op jit(solution)/shard_map/ppermute | solution.py:234
  3.0 13.0 %collective-permute-start.3 = (bf16[384,384]{1,0:T(8,128)(2,1)}, bf16[384,384]{1,0:T(8,128)(2,1)S(1)}, u32[]{:S(2)}, u32[]{:S(2)}) collective-permute-start(bf16[384,384]{1,0:T(8,128)(2,1)} %bitcast.10), channel_id=1, source_target_pairs={{4,0},{16,4},{12,8},{24,12},{20,16},{0,20},{28,24},{8,28},{5,1},{1... | collective-permute-start | bytes 884744 | tf_op jit(solution)/shard_map/ppermute | solution.py:234
  5.0 6.8 %collective-permute-start.2 = (bf16[16,384]{1,0:T(8,128)(2,1)S(1)}, bf16[16,384]{1,0:T(8,128)(2,1)S(1)}, u32[]{:S(2)}, u32[]{:S(2)}) collective-permute-start(bf16[16,384]{1,0:T(8,128)(2,1)S(1)} %turn.1.own_turn), channel_id=1, source_target_pairs={{8,0},{12,4},{16,8},{20,12},{24,16},{28,20},{0,24},{4,28},{9,1},{1... | collective-permute-start | bytes 36872 | tf_op jit(solution)/shard_map/ppermute | solution.py:234
  7.2 10.3 %collective-permute-start.5 = (bf16[16,384]{1,0:T(8,128)(2,1)S(1)}, bf16[16,384]{1,0:T(8,128)(2,1)S(1)}, u32[]{:S(2)}, u32[]{:S(2)}) collective-permute-start(bf16[16,384]{1,0:T(8,128)(2,1)S(1)} %turn.1.own_turn), channel_id=1, source_target_pairs={{4,0},{16,4},{12,8},{24,12},{20,16},{0,20},{28,24},{8,28},{5,1},{1... | collective-permute-start | bytes 36872 | tf_op jit(solution)/shard_map/ppermute | solution.py:234
  11.8 4.3 %copy-start.1 = (bf16[64,464]{1,0:T(8,128)(2,1)S(1)}, bf16[64,464]{1,0:T(8,128)(2,1)}, u32[]{:S(2)}) copy-start(bf16[64,464]{1,0:T(8,128)(2,1)} %constant.10.clone.rows_back) | copy-start | bytes 178180
  13.2 4.3 %collective-permute-start.4 = (bf16[480,768]{1,0:T(8,128)(2,1)S(1)}, bf16[480,768]{1,0:T(8,128)(2,1)S(1)}, u32[]{:S(2)}, u32[]{:S(2)}) collective-permute-start(bf16[480,768]{1,0:T(8,128)(2,1)S(1)} %get-tuple-element.31.far_packed), channel_id=1, source_target_pairs={{4,0},{0,4},{12,8},{8,12},{20,16},{16,20},{28,24},{24,28},{5,1},{1... | collective-permute-start | bytes 2211848 | tf_op jit(solution)/shard_map/ppermute | solution.py:234
  16.1 1.5 %copy-start = (bf16[768,384]{1,0:T(8,128)(2,1)S(1)}, bf16[768,384]{1,0:T(8,128)(2,1)}, u32[]{:S(2)}) copy-start(bf16[768,384]{1,0:T(8,128)(2,1)} %constant.11.clone.cols_back) | copy-start | bytes 1769476

commit v3 on v2

--- a/solution.py
+++ b/solution.py
@@ -27,7 +27,7 @@
 BASE_DEFOCUS = 8000.0
 DEFOCUS_STEP = 1000.0
 
-COST = (10**5, 10**5, 10**5, 10**10, 10**5)
+COST = (10**5, 10**5, 10**5, 10**5, 10**10, 10**5)
 
 HBM = pl.BlockSpec(memory_space=pltpu.HBM)
 SMEM = pl.BlockSpec(memory_space=pltpu.SMEM)
@@ -158,14 +158,16 @@
     back[...] = dot(rows_back[...], product[...]).astype(jnp.bfloat16)
 
 
-def second_kernel(far, halo, far_turn, own_part, ctf, rows, cols, far_packed, micro):
-    far_half = dot(rows[:, :TS], far[...]).astype(jnp.bfloat16)
+def far_kernel(far, far_turn, rows, cols, far_packed):
+    far_packed[:ROWS, :] = spectrum_of(far, rows, cols)
+    far_packed[ROWS:, :HALF] = far_turn[...]
+    far_packed[ROWS:, HALF:] = far_turn[...]
+
+
+def strip_spectrum(halo, own_part, ctf, rows, cols, micro):
     halo_half = dot(rows[:, :MR], halo[...])
     lanes = lax.broadcasted_iota(jnp.int32, halo_half.shape, 1)
     halo_half = jnp.where(lanes < TC - 1, halo_half, 0.0).astype(jnp.bfloat16)
-    far_packed[:ROWS, :] = dot(far_half, cols[...]).astype(jnp.bfloat16)
-    far_packed[ROWS:, :HALF] = far_turn[...]
-    far_packed[ROWS:, HALF:] = far_turn[...]
     lanes = lax.broadcasted_iota(jnp.int32, (1, 2 * HALF), 1)
     signs = jnp.where(lanes % 2 == 0, 1.0, -1.0)
     m_a, m_b, m_d, m_e, m_x, m_y = blocks(own_part[...] + signs * dot(halo_half, cols[...]))
@@ -178,18 +180,65 @@
     micro[LR:, HALF:] = -(ctf_edge * m_y)
 
 
+def waits_long(choice):
+    return pl.when((lax.axis_index("mic") % 4 == 3) == choice)
+
+
+def early_strip_kernel(
+    halo, own_part, ctf, rows, cols, own_spectrum, rows_back, micro, back, product
+):
+    @waits_long(True)
+    def _():
+        strip_spectrum(halo, own_part, ctf, rows, cols, micro)
+        multiply_back(micro, own_spectrum, rows_back, product, back)
+
+
+def strip_kernel(
+    halo,
+    own_part,
+    ctf,
+    rows,
+    cols,
+    own_spectrum,
+    rows_back,
+    far_packed,
+    early_micro,
+    early_back,
+    micro,
+    back_own,
+    back_far,
+    product,
+):
+    @waits_long(False)
+    def _():
+        strip_spectrum(halo, own_part, ctf, rows, cols, micro)
+        multiply_back(micro, own_spectrum, rows_back, product, back_own)
+
+    @waits_long(True)
+    def _():
+        micro[...] = early_micro[...]
+        back_own[...] = early_back[...]
+        multiply_back(early_micro, far_packed, rows_back, product, back_far)
+
+
 def third_kernel(
-    near, micro, own_spectrum, far_packed, rows, cols, rows_back, near_spectrum, back_early, products
-):
-    near_half = dot(rows[:, :TS], near[...]).astype(jnp.bfloat16)
-    multiply_back(micro, own_spectrum, rows_back, products.at[0], back_early.at[:MH])
-    near_spectrum[...] = dot(near_half, cols[...]).astype(jnp.bfloat16)
-    multiply_back(micro, far_packed, rows_back, products.at[1], back_early.at[MH:])
+    near, micro, far_packed, rows, cols, rows_back, early_far, near_spectrum, back, product
+):
+    @waits_long(False)
+    def _():
+        near_spectrum[...] = spectrum_of(near, rows, cols)
+        multiply_back(micro, far_packed, rows_back, product, back)
+
+    @waits_long(True)
+    def _():
+        near_spectrum[...] = spectrum_of(near, rows, cols)
+        back[...] = early_far[...]
 
 
 def last_kernel(
     micro,
-    back_early,
+    back_own,
+    back_far,
     near_spectrum,
     late_packed,
     own_turn,
@@ -203,13 +252,15 @@
     orient_cos,
     orient_sin,
     products,
-    back_late,
-):
-    multiply_back(micro, near_spectrum, rows_back, products.at[0], back_late.at[:MH])
-    multiply_back(micro, late_packed, rows_back, products.at[1], back_late.at[MH:])
+    back_all,
+):
+    back_all[:MH, :] = back_own[...]
+    back_all[MH : 2 * MH, :] = back_far[...]
+    multiply_back(micro, near_spectrum, rows_back, products.at[0], back_all.at[2 * MH : 3 * MH])
+    multiply_back(micro, late_packed, rows_back, products.at[1], back_all.at[3 * MH :])
     scale = 1.0 / (TS * LR * LC)
-    halves = [dot(back[...], cols_back[...]) * scale for back in (back_early, back_late)]
-    corrs = [half[step * MH : (step + 1) * MH, :] for half in halves for step in range(2)]
+    corr_all = dot(back_all[...], cols_back[...]) * scale
+    corrs = [corr_all[step * MH : (step + 1) * MH, :] for step in range(STEPS)]
     turns = (own_turn[...], far_packed[ROWS:, :HALF], near_turn[...], late_packed[ROWS:, :HALF])
     sums = None
     for corr, turn in zip(corrs, turns):
@@ -287,36 +338,45 @@
         [pltpu.VMEM((MR, TC), bf16), pltpu.SemaphoreType.DMA((4,))],
     )(defocus_bins, *own_inputs)
     near = along(own, near_places)
-    far, halo, own_spectrum = lax.optimization_barrier((far, halo, own_spectrum))
-    far_packed, micro = call(
-        second_kernel,
-        "far_and_strip",
+    far, own_spectrum = lax.optimization_barrier((far, own_spectrum))
+    back_type = jax.ShapeDtypeStruct((MH, 2 * HALF), bf16)
+    strip_types = (jax.ShapeDtypeStruct((ROWS, 2 * HALF), f32), back_type)
+    far_packed = call(
+        far_kernel,
+        "far_spectrum",
         COST[2],
-        (
-            jax.ShapeDtypeStruct((ROWS + EDGE, 2 * HALF), bf16),
-            jax.ShapeDtypeStruct((ROWS, 2 * HALF), f32),
-        ),
+        jax.ShapeDtypeStruct((ROWS + EDGE, 2 * HALF), bf16),
+        [VMEM] * 4,
+    )(far, far_turn, rows, cols)
+    strip_inputs = (halo, own_part, ctf, rows, cols, own_spectrum, rows_back)
+    product_scratch = [pltpu.VMEM((ROWS, 2 * HALF), bf16)]
+    early_micro, early_back = call(
+        early_strip_kernel, "early_strip", COST[3], strip_types, [VMEM] * 7, product_scratch
+    )(*strip_inputs)
+    far_packed, early_micro = lax.optimization_barrier((far_packed, early_micro))
+    late_packed = along(far_packed, [d ^ 1 for d in range(count)])
+    micro, back_own, early_far = call(
+        strip_kernel, "strip", COST[3], (*strip_types, back_type), [VMEM] * 10, product_scratch
+    )(*strip_inputs, far_packed, early_micro, early_back)
+    near_spectrum, back_far = call(
+        third_kernel,
+        "near_and_far",
+        COST[4],
+        (spectrum_type, back_type),
         [VMEM] * 7,
-    )(far, halo, far_turn, own_part, ctf, rows, cols)
-    late_packed = along(far_packed, [d ^ 1 for d in range(count)])
-    near_spectrum, back_early = call(
-        third_kernel,
-        "near_and_early",
-        COST[3],
-        (spectrum_type, jax.ShapeDtypeStruct((2 * MH, 2 * HALF), bf16)),
-        [VMEM] * 7,
-        [pltpu.VMEM((2, ROWS, 2 * HALF), bf16)],
-    )(near, micro, own_spectrum, far_packed, rows, cols, rows_back)
+        product_scratch,
+    )(near, micro, far_packed, rows, cols, rows_back, early_far)
     results = call(
         last_kernel,
         "match",
-        COST[4],
+        COST[5],
         (jax.ShapeDtypeStruct((MH, TC), f32),) * 5,
-        [VMEM] * 9,
-        [pltpu.VMEM((2, ROWS, 2 * HALF), bf16), pltpu.VMEM((2 * MH, 2 * HALF), bf16)],
+        [VMEM] * 10,
+        [pltpu.VMEM((2, ROWS, 2 * HALF), bf16), pltpu.VMEM((STEPS * MH, 2 * HALF), bf16)],
     )(
         micro,
-        back_early,
+        back_own,
+        back_far,
         near_spectrum,
         late_packed,
         own_turn,

time: 20.1 us -> 19.7 us (0.980)
  starting transfers between devices: 8.13 us -> 6.66 us
  Pallas kernels: 8.17 us -> 9.3 us
    ppermute x5, starting transfers between devices: 6.04 us -> 4.57 us  [along(): lax.ppermute(array, 'mic', [(source, place) for place, source in enumerat...]
    pallas_call x3 -> x5, Pallas kernels: 5.18 us -> 6.3 us  [the longest x1 2.35 us: body(): call(last_kernel, 'match', COST[5], (jax.ShapeDtypeStruct((MH, TC), f32),...]
  transfers between devices with their start and end apart: 6 -> 6, of which waited for: 3 -> 3; matrix products, arithmetic and copies ran while one was open for 0% -> 0% of each run, Pallas kernels for 30% -> 36%
where the time goes in v3:
time: 19.7 us; the launch traced here: 19.5 us
  Pallas kernels  9.3 us (47%)
  starting transfers between devices  6.66 us (34%)
  between operations  2.02 us (10%)
  waiting for transfers between devices  1.33 us (7%)
    ppermute x5, starting transfers between devices, along(): lax.ppermute(array, 'mic', [(source, place) for place, source in enumerat...  4.57 us
    pallas_call x1, Pallas kernels, body(): call(first_kernel, 'own_spectra', COST[1], (jax.ShapeDtypeStruct(rows_far...  2.95 us
    pallas_call x1, Pallas kernels, body(): call(last_kernel, 'match', COST[5], (jax.ShapeDtypeStruct((MH, TC), f32),...  2.35 us
    ppermute x1, starting transfers between devices, body(): halo = lax.ppermute(strip, 'tile', [(i + 1, i) for i in range(tiles - 1)])  2.1 us
    pallas_call x1, Pallas kernels, body(): call(early_strip_kernel, 'early_strip', COST[3], strip_types, [VMEM] * 7,...  1.49 us
    ppermute x5, waiting for transfers between devices, along(): lax.ppermute(array, 'mic', [(source, place) for place, source in enumerat...  1.33 us
    pallas_call x1, Pallas kernels, body(): call(far_kernel, 'far_spectrum', COST[2], jax.ShapeDtypeStruct((ROWS + ED...  0.9 us
    pallas_call x1, Pallas kernels, body(): call(third_kernel, 'near_and_far', COST[4], (spectrum_type, back_type), [...  0.89 us
  transfers between devices with their start and end apart: 6, of which 3 were waited for; matrix products, arithmetic and copies ran while one was open for 0% of the time, Pallas kernels for 36%

profile of v3, /device:TPU:27, one launch (start us, length us, event | category | flops | bytes accessed | tf_op | source)
XLA Modules:
  0.0 19.5 jit_solution(2178409416241697232)
XLA Ops:
  0.6 2.1 %collective-permute-start = (bf16[447,384]{1,0:T(8,128)(2,1)}, bf16[447,384]{1,0:T(8,128)(2,1)S(1)}, u32[]{:S(2)}, u32[]{:S(2)}) collective-permute-start(bf16[447,384]{1,0:T(8,128)(2,1)} %bitcast.7), channel_id=1, source_target_pairs={{1,0},{2,1},{3,2},{5,4},{6,5},{7,6},{9,8},{10,9},{11,10},{13,12},{... | collective-permute-start | bytes 1029896 | tf_op jit(solution)/shard_map/ppermute | solution.py:313
  2.7 0.3 %collective-permute-start.1 = (bf16[384,384]{1,0:T(8,128)(2,1)}, bf16[384,384]{1,0:T(8,128)(2,1)S(1)}, u32[]{:S(2)}, u32[]{:S(2)}) collective-permute-start(bf16[384,384]{1,0:T(8,128)(2,1)} %bitcast.9), channel_id=1, source_target_pairs={{8,0},{12,4},{16,8},{20,12},{24,16},{28,20},{0,24},{4,28},{9,1},{1... | collective-permute-start | bytes 884744 | tf_op jit(solution)/shard_map/ppermute | solution.py:285
  3.0 1.2 %collective-permute-start.3 = (bf16[384,384]{1,0:T(8,128)(2,1)}, bf16[384,384]{1,0:T(8,128)(2,1)S(1)}, u32[]{:S(2)}, u32[]{:S(2)}) collective-permute-start(bf16[384,384]{1,0:T(8,128)(2,1)} %bitcast.10), channel_id=1, source_target_pairs={{4,0},{16,4},{12,8},{24,12},{20,16},{0,20},{28,24},{8,28},{5,1},{1... | collective-permute-start | bytes 884744 | tf_op jit(solution)/shard_map/ppermute | solution.py:285
  5.0 2.2 %collective-permute-start.2 = (bf16[16,384]{1,0:T(8,128)(2,1)S(1)}, bf16[16,384]{1,0:T(8,128)(2,1)S(1)}, u32[]{:S(2)}, u32[]{:S(2)}) collective-permute-start(bf16[16,384]{1,0:T(8,128)(2,1)S(1)} %turn.1.own_turn), channel_id=1, source_target_pairs={{8,0},{12,4},{16,8},{20,12},{24,16},{28,20},{0,24},{4,28},{9,1},{1... | collective-permute-start | bytes 36872 | tf_op jit(solution)/shard_map/ppermute | solution.py:285
  7.2 0.3 %collective-permute-start.5 = (bf16[16,384]{1,0:T(8,128)(2,1)S(1)}, bf16[16,384]{1,0:T(8,128)(2,1)S(1)}, u32[]{:S(2)}, u32[]{:S(2)}) collective-permute-start(bf16[16,384]{1,0:T(8,128)(2,1)S(1)} %turn.1.own_turn), channel_id=1, source_target_pairs={{4,0},{16,4},{12,8},{24,12},{20,16},{0,20},{28,24},{8,28},{5,1},{1... | collective-permute-start | bytes 36872 | tf_op jit(solution)/shard_map/ppermute | solution.py:285
  8.1 3.0 %own_spectra.1 = (bf16[464,448]{1,0:T(8,128)(2,1)S(1)}, bf16[384,768]{1,0:T(8,128)(2,1)S(1)}, bf16[384,384]{1,0:T(8,128)(2,1)}, f32[464,768]{1,0:T(8,128)S(1)}, ...) custom-call(s32[1]{0:T(128)S(6)} %copy.14.bins, bf16[447,384]{1,0:T(8,128)(2,1)} %bitcast.8, ...), custom_call_target="tpu_custom_call" | custom-call | flops 100000 | bytes 1000 | tf_op jit(solution)/shard_map/own_spectra/pallas_call | solution.py:325
  11.1 0.0 copy-start
  11.1 0.4 %collective-permute-done.1.far = bf16[384,384]{1,0:T(8,128)(2,1)S(1)} collective-permute-done((bf16[384,384]{1,0:T(8,128)(2,1)}, bf16[384,384]{1,0:T(8,128)(2,1)S(1)}, u32[]{:S(2)}, u32[]{:S(2)}) %collective-permute-start.1) | collective-permute-done | bytes 294944 | tf_op jit(solution)/shard_map/ppermute | solution.py:285
  11.5 0.3 %collective-permute-done.2.far_turn = bf16[16,384]{1,0:T(8,128)(2,1)S(1)} collective-permute-done((bf16[16,384]{1,0:T(8,128)(2,1)S(1)}, bf16[16,384]{1,0:T(8,128)(2,1)S(1)}, u32[]{:S(2)}, u32[]{:S(2)}) %collective-permute-start.2) | collective-permute-done | bytes 12320 | tf_op jit(solution)/shard_map/ppermute | solution.py:285
  11.8 0.9 %far_spectrum.1.far_packed = bf16[480,768]{1,0:T(8,128)(2,1)S(1)} custom-call(bf16[384,384]{1,0:T(8,128)(2,1)S(1)} %collective-permute-done.1.far, bf16[16,384]{1,0:T(8,128)(2,1)S(1)} %collective-permute-done.2.far_turn, bf16[464,448]{1,0:T(8,128)(2,1)S(1)} %get-tuple-element.28.rows, bf16[384,768]{1,0:T(8,128)(2,1)S(1)} %get-tuple-element.29.cols), custom_call_target="tpu_custom_call" | custom-call | flops 100000 | bytes 1000 | tf_op jit(solution)/shard_map/far_spectrum/pallas_call | solution.py:344
  12.7 0.0 collective-permute-done.halo
  12.7 0.0 copy-done
  12.7 1.5 %early_strip.1 = (f32[464,768]{1,0:T(8,128)S(1)}, bf16[64,768]{1,0:T(8,128)(2,1)S(1)}) custom-call(bf16[447,384]{1,0:T(8,128)(2,1)S(1)} %collective-permute-done.halo, f32[464,768]{1,0:T(8,128)S(1)} %get-tuple-element.26.own_part, f32[240,384]{1,0:T(8,128)S(1)} %get-tuple-element.27.ctf, bf16[464,448]{1,0:T(8,128)(2,1)S(1)} %get-tuple-element.28.rows, ...), custom_call_target="tpu_custom_call" | custom-call | flops 100000 | bytes 1000 | tf_op jit(solution)/shard_map/early_strip/pallas_call | solution.py:353
  14.2 0.5 %collective-permute-start.4 = (bf16[480,768]{1,0:T(8,128)(2,1)S(1)}, bf16[480,768]{1,0:T(8,128)(2,1)S(1)}, u32[]{:S(2)}, u32[]{:S(2)}) collective-permute-start(bf16[480,768]{1,0:T(8,128)(2,1)S(1)} %far_spectrum.1.far_packed), channel_id=1, source_target_pairs={{4,0},{0,4},{12,8},{8,12},{20,16},{16,20},{28,24},{24,28},{5,1},{1... | collective-permute-start | bytes 2211848 | tf_op jit(solution)/shard_map/ppermute | solution.py:285
  14.7 0.7 %strip.1 = (f32[464,768]{1,0:T(8,128)S(1)}, bf16[64,768]{1,0:T(8,128)(2,1)S(1)}, bf16[64,768]{1,0:T(8,128)(2,1)S(1)}) custom-call(bf16[447,384]{1,0:T(8,128)(2,1)S(1)} %collective-permute-done.halo, f32[464,768]{1,0:T(8,128)S(1)} %get-tuple-element.26.own_part, f32[240,384]{1,0:T(8,128)S(1)} %get-tuple-element.27.ctf, ...), custom_call_target="tpu_custom_call" | custom-call | flops 100000 | bytes 1000 | tf_op jit(solution)/shard_map/strip/pallas_call | solution.py:358
  15.4 0.7 %collective-permute-done.3.near = bf16[384,384]{1,0:T(8,128)(2,1)S(1)} collective-permute-done((bf16[384,384]{1,0:T(8,128)(2,1)}, bf16[384,384]{1,0:T(8,128)(2,1)S(1)}, u32[]{:S(2)}, u32[]{:S(2)}) %collective-permute-start.3) | collective-permute-done | bytes 294944 | tf_op jit(solution)/shard_map/ppermute | solution.py:285
  16.1 0.0 copy-start.1
  16.1 0.9 %near_and_far.1 = (bf16[464,768]{1,0:T(8,128)(2,1)S(1)}, bf16[64,768]{1,0:T(8,128)(2,1)S(1)}) custom-call(bf16[384,384]{1,0:T(8,128)(2,1)S(1)} %collective-permute-done.3.near, f32[464,768]{1,0:T(8,128)S(1)} %get-tuple-element.37.micro, bf16[480,768]{1,0:T(8,128)(2,1)S(1)} %far_spectrum.1.far_packed, bf16[464,448]{1,0:T(8,128)(2,1)S(1)} %get-tuple-element.28.rows, ...), custom_call_target="tpu_custom_call" | custom-call | flops 10000000000 | bytes 1000 | tf_op jit(solution)/shard_map/near_and_far/pallas_call | solution.py:361
  17.0 0.0 collective-permute-done.5.near_turn
  17.0 0.0 collective-permute-done.4.late_packed
  17.0 0.1 copy-done.1
  17.1 2.3 %match.1 = (f32[64,384]{1,0:T(8,128)}, f32[64,384]{1,0:T(8,128)}, f32[64,384]{1,0:T(8,128)}, f32[64,384]{1,0:T(8,128)}, f32[64,384]{1,0:T(8,128)}) custom-call(f32[464,768]{1,0:T(8,128)S(1)} %get-tuple-element.37.micro, bf16[64,768]{1,0:T(8,128)(2,1)S(1)} %get-tuple-element.38.back_own, bf16[64,768]{1,0:T(8,128)(2,1)S(1)} %get-tuple-element.40.back_far, ...), custom_call_target="tpu_custom_call" | custom-call | flops 100000 | bytes 1000 | tf_op jit(solution)/shard_map/match/pallas_call | solution.py:369
  (1 shorter events, 0.0 us)
Async XLA Ops:
  0.6 12.0 %collective-permute-start = (bf16[447,384]{1,0:T(8,128)(2,1)}, bf16[447,384]{1,0:T(8,128)(2,1)S(1)}, u32[]{:S(2)}, u32[]{:S(2)}) collective-permute-start(bf16[447,384]{1,0:T(8,128)(2,1)} %bitcast.7), channel_id=1, source_target_pairs={{1,0},{2,1},{3,2},{5,4},{6,5},{7,6},{9,8},{10,9},{11,10},{13,12},{... | collective-permute-start | bytes 1029896 | tf_op jit(solution)/shard_map/ppermute | solution.py:313
  2.7 8.8 %collective-permute-start.1 = (bf16[384,384]{1,0:T(8,128)(2,1)}, bf16[384,384]{1,0:T(8,128)(2,1)S(1)}, u32[]{:S(2)}, u32[]{:S(2)}) collective-permute-start(bf16[384,384]{1,0:T(8,128)(2,1)} %bitcast.9), channel_id=1, source_target_pairs={{8,0},{12,4},{16,8},{20,12},{24,16},{28,20},{0,24},{4,28},{9,1},{1... | collective-permute-start | bytes 884744 | tf_op jit(solution)/shard_map/ppermute | solution.py:285
  3.0 13.0 %collective-permute-start.3 = (bf16[384,384]{1,0:T(8,128)(2,1)}, bf16[384,384]{1,0:T(8,128)(2,1)S(1)}, u32[]{:S(2)}, u32[]{:S(2)}) collective-permute-start(bf16[384,384]{1,0:T(8,128)(2,1)} %bitcast.10), channel_id=1, source_target_pairs={{4,0},{16,4},{12,8},{24,12},{20,16},{0,20},{28,24},{8,28},{5,1},{1... | collective-permute-start | bytes 884744 | tf_op jit(solution)/shard_map/ppermute | solution.py:285
  5.0 6.8 %collective-permute-start.2 = (bf16[16,384]{1,0:T(8,128)(2,1)S(1)}, bf16[16,384]{1,0:T(8,128)(2,1)S(1)}, u32[]{:S(2)}, u32[]{:S(2)}) collective-permute-start(bf16[16,384]{1,0:T(8,128)(2,1)S(1)} %turn.1.own_turn), channel_id=1, source_target_pairs={{8,0},{12,4},{16,8},{20,12},{24,16},{28,20},{0,24},{4,28},{9,1},{1... | collective-permute-start | bytes 36872 | tf_op jit(solution)/shard_map/ppermute | solution.py:285
  7.2 9.8 %collective-permute-start.5 = (bf16[16,384]{1,0:T(8,128)(2,1)S(1)}, bf16[16,384]{1,0:T(8,128)(2,1)S(1)}, u32[]{:S(2)}, u32[]{:S(2)}) collective-permute-start(bf16[16,384]{1,0:T(8,128)(2,1)S(1)} %turn.1.own_turn), channel_id=1, source_target_pairs={{4,0},{16,4},{12,8},{24,12},{20,16},{0,20},{28,24},{8,28},{5,1},{1... | collective-permute-start | bytes 36872 | tf_op jit(solution)/shard_map/ppermute | solution.py:285
  11.1 1.6 %copy-start = (bf16[64,464]{1,0:T(8,128)(2,1)S(1)}, bf16[64,464]{1,0:T(8,128)(2,1)}, u32[]{:S(2)}) copy-start(bf16[64,464]{1,0:T(8,128)(2,1)} %constant.10.clone.rows_back) | copy-start | bytes 178180
  14.2 2.8 %collective-permute-start.4 = (bf16[480,768]{1,0:T(8,128)(2,1)S(1)}, bf16[480,768]{1,0:T(8,128)(2,1)S(1)}, u32[]{:S(2)}, u32[]{:S(2)}) collective-permute-start(bf16[480,768]{1,0:T(8,128)(2,1)S(1)} %far_spectrum.1.far_packed), channel_id=1, source_target_pairs={{4,0},{0,4},{12,8},{8,12},{20,16},{16,20},{28,24},{24,28},{5,1},{1... | collective-permute-start | bytes 2211848 | tf_op jit(solution)/shard_map/ppermute | solution.py:285
  16.1 1.1 %copy-start.1 = (bf16[768,384]{1,0:T(8,128)(2,1)S(1)}, bf16[768,384]{1,0:T(8,128)(2,1)}, u32[]{:S(2)}) copy-start(bf16[768,384]{1,0:T(8,128)(2,1)} %constant.11.clone.cols_back) | copy-start | bytes 1769476

commit v4 on v3

--- a/solution.py
+++ b/solution.py
@@ -64,9 +64,15 @@
     return jnp.dot(left, right, preferred_element_type=jnp.float32)
 
 
-def spectrum_of(template, rows, cols):
+def store_spectrum(target, template, rows, cols):
     half_way = dot(rows[:, :TS], template[...]).astype(jnp.bfloat16)
-    return dot(half_way, cols[...]).astype(jnp.bfloat16)
+    t_a, t_b, t_d, t_e, t_x, t_y = blocks(dot(half_way, cols[...]))
+    target[:PAIRS, :HALF] = (t_a - t_e).astype(jnp.bfloat16)
+    target[:PAIRS, HALF:] = (t_b + t_d).astype(jnp.bfloat16)
+    target[PAIRS:LR, :HALF] = (t_a + t_e).astype(jnp.bfloat16)
+    target[PAIRS:LR, HALF:] = (t_b - t_d).astype(jnp.bfloat16)
+    target[LR:ROWS, :HALF] = t_x.astype(jnp.bfloat16)
+    target[LR:ROWS, HALF:] = t_y.astype(jnp.bfloat16)
 
 
 def turn_kernel(orient_id, turn):
@@ -80,8 +86,12 @@
     template_far,
     rows_far,
     cols_far,
+    rows_back_far,
+    cols_back_far,
     rows,
     cols,
+    rows_back,
+    cols_back,
     template,
     own_part,
     ctf,
@@ -94,6 +104,8 @@
         (cols_far, cols),
         (template_far, template),
         (strip_far, strip),
+        (rows_back_far, rows_back),
+        (cols_back_far, cols_back),
     )
     copies = [
         pltpu.make_async_copy(source, target, arrived.at[i])
@@ -115,7 +127,7 @@
     ctf[...] = values * jnp.where(row_ids == 0, 0.5, 1.0)
     for copy in copies:
         copy.wait()
-    spectrum[...] = spectrum_of(template, rows, cols)
+    store_spectrum(spectrum, template, rows, cols)
     half_way = dot(rows[:, :MR], strip[...]).astype(jnp.bfloat16)
     own_part[...] = dot(half_way, cols[...])
 
@@ -134,14 +146,12 @@
         up, down = slice(row, row + EDGE), slice(PAIRS + row, PAIRS + row + EDGE)
         for col in range(0, HALF, 128):
             real, imag = slice(col, col + 128), slice(HALF + col, HALF + col + 128)
-            t_a, t_b, t_d, t_e = (
+            s_real, s_imag, r_real, r_imag = (
                 spectrum[place].astype(jnp.float32)
                 for place in ((up, real), (up, imag), (down, real), (down, imag))
             )
             up_real, up_imag = micro[up, real], micro[up, imag]
             down_real, down_imag = micro[down, real], micro[down, imag]
-            s_real, s_imag = t_a - t_e, t_b + t_d
-            r_real, r_imag = t_a + t_e, t_b - t_d
             p_real = up_real * s_real - up_imag * s_imag
             p_imag = up_real * s_imag + up_imag * s_real
             q_real = down_real * r_real - down_imag * r_imag
@@ -159,7 +169,7 @@
 
 
 def far_kernel(far, far_turn, rows, cols, far_packed):
-    far_packed[:ROWS, :] = spectrum_of(far, rows, cols)
+    store_spectrum(far_packed, far, rows, cols)
     far_packed[ROWS:, :HALF] = far_turn[...]
     far_packed[ROWS:, HALF:] = far_turn[...]
 
@@ -226,12 +236,12 @@
 ):
     @waits_long(False)
     def _():
-        near_spectrum[...] = spectrum_of(near, rows, cols)
+        store_spectrum(near_spectrum, near, rows, cols)
         multiply_back(micro, far_packed, rows_back, product, back)
 
     @waits_long(True)
     def _():
-        near_spectrum[...] = spectrum_of(near, rows, cols)
+        store_spectrum(near_spectrum, near, rows, cols)
         back[...] = early_far[...]
 
 
@@ -301,8 +311,8 @@
 def body(micrograph, templates, orient_ids, defocus_bins):
     rows_far = jnp.asarray(paired_rows())
     cols_far = jnp.asarray(forward_columns())
-    rows_back = jnp.asarray(np.ascontiguousarray(paired_rows()[:, :MH].T))
-    cols_back = jnp.asarray(inverse_columns())
+    rows_back_far = jnp.asarray(np.ascontiguousarray(paired_rows()[:, :MH].T))
+    cols_back_far = jnp.asarray(inverse_columns())
     count = lax.axis_size("mic")
     tiles = lax.axis_size("tile")
     strip = micrograph[0]
@@ -320,22 +330,24 @@
     bf16, f32 = jnp.bfloat16, jnp.float32
     spectrum_type = jax.ShapeDtypeStruct((ROWS, 2 * HALF), bf16)
     own_inputs = [
-        pltpu.with_memory_space_constraint(x, pltpu.HBM) for x in (strip, own, rows_far, cols_far)
+        pltpu.with_memory_space_constraint(x, pltpu.HBM) for x in (strip, own, rows_far, cols_far, rows_back_far, cols_back_far)
     ]
-    rows, cols, template, own_part, ctf, own_spectrum = call(
+    rows, cols, rows_back, cols_back, template, own_part, ctf, own_spectrum = call(
         first_kernel,
         "own_spectra",
         COST[1],
         (
             jax.ShapeDtypeStruct(rows_far.shape, bf16),
             jax.ShapeDtypeStruct(cols_far.shape, bf16),
+            jax.ShapeDtypeStruct(rows_back_far.shape, bf16),
+            jax.ShapeDtypeStruct(cols_back_far.shape, bf16),
             jax.ShapeDtypeStruct(own.shape, bf16),
             jax.ShapeDtypeStruct((ROWS, 2 * HALF), f32),
             jax.ShapeDtypeStruct((PAIRS + EDGE, HALF), f32),
             spectrum_type,
         ),
-        [SMEM] + [HBM] * 4,
-        [pltpu.VMEM((MR, TC), bf16), pltpu.SemaphoreType.DMA((4,))],
+        [SMEM] + [HBM] * 6,
+        [pltpu.VMEM((MR, TC), bf16), pltpu.SemaphoreType.DMA((6,))],
     )(defocus_bins, *own_inputs)
     near = along(own, near_places)
     far, own_spectrum = lax.optimization_barrier((far, own_spectrum))

time: 19.7 us -> 19.5 us (0.990)
    pallas_call x1, Pallas kernels: 2.95 us -> 3.18 us  [body(): call(first_kernel, 'own_spectra', COST[1], (jax.ShapeDtypeStruct(rows_far...]
  transfers between devices with their start and end apart: 6 -> 6, of which waited for: 3 -> 3; matrix products, arithmetic and copies ran while one was open for 0% -> 0% of each run, Pallas kernels for 36% -> 37%
where the time goes in v4:
time: 19.5 us; the launch traced here: 19.3 us
  Pallas kernels  9.48 us (49%)
  starting transfers between devices  6.66 us (34%)
  between operations  2.01 us (10%)
  waiting for transfers between devices  1.16 us (6%)
    ppermute x5, starting transfers between devices, along(): lax.ppermute(array, 'mic', [(source, place) for place, source in enumerat...  4.57 us
    pallas_call x1, Pallas kernels, body(): call(first_kernel, 'own_spectra', COST[1], (jax.ShapeDtypeStruct(rows_far...  3.18 us
    pallas_call x1, Pallas kernels, body(): call(last_kernel, 'match', COST[5], (jax.ShapeDtypeStruct((MH, TC), f32),...  2.33 us
    ppermute x1, starting transfers between devices, body(): halo = lax.ppermute(strip, 'tile', [(i + 1, i) for i in range(tiles - 1)])  2.1 us
    pallas_call x1, Pallas kernels, body(): call(early_strip_kernel, 'early_strip', COST[3], strip_types, [VMEM] * 7,...  1.49 us
    ppermute x5, waiting for transfers between devices, along(): lax.ppermute(array, 'mic', [(source, place) for place, source in enumerat...  1.16 us
    pallas_call x1, Pallas kernels, body(): call(far_kernel, 'far_spectrum', COST[2], jax.ShapeDtypeStruct((ROWS + ED...  0.9 us
    pallas_call x1, Pallas kernels, body(): call(third_kernel, 'near_and_far', COST[4], (spectrum_type, back_type), [...  0.89 us
  transfers between devices with their start and end apart: 6, of which 3 were waited for; matrix products, arithmetic and copies ran while one was open for 0% of the time, Pallas kernels for 37%

profile of v4, /device:TPU:27, one launch (start us, length us, event | category | flops | bytes accessed | tf_op | source)
XLA Modules:
  0.0 19.3 jit_solution(17915345564480021873)
XLA Ops:
  0.6 2.1 %collective-permute-start = (bf16[447,384]{1,0:T(8,128)(2,1)}, bf16[447,384]{1,0:T(8,128)(2,1)S(1)}, u32[]{:S(2)}, u32[]{:S(2)}) collective-permute-start(bf16[447,384]{1,0:T(8,128)(2,1)} %bitcast.7), channel_id=1, source_target_pairs={{1,0},{2,1},{3,2},{5,4},{6,5},{7,6},{9,8},{10,9},{11,10},{13,12},{... | collective-permute-start | bytes 1029896 | tf_op jit(solution)/shard_map/ppermute | solution.py:323
  2.7 0.3 %collective-permute-start.1 = (bf16[384,384]{1,0:T(8,128)(2,1)}, bf16[384,384]{1,0:T(8,128)(2,1)S(1)}, u32[]{:S(2)}, u32[]{:S(2)}) collective-permute-start(bf16[384,384]{1,0:T(8,128)(2,1)} %bitcast.9), channel_id=1, source_target_pairs={{8,0},{12,4},{16,8},{20,12},{24,16},{28,20},{0,24},{4,28},{9,1},{1... | collective-permute-start | bytes 884744 | tf_op jit(solution)/shard_map/ppermute | solution.py:295
  3.0 1.2 %collective-permute-start.3 = (bf16[384,384]{1,0:T(8,128)(2,1)}, bf16[384,384]{1,0:T(8,128)(2,1)S(1)}, u32[]{:S(2)}, u32[]{:S(2)}) collective-permute-start(bf16[384,384]{1,0:T(8,128)(2,1)} %bitcast.10), channel_id=1, source_target_pairs={{4,0},{16,4},{12,8},{24,12},{20,16},{0,20},{28,24},{8,28},{5,1},{1... | collective-permute-start | bytes 884744 | tf_op jit(solution)/shard_map/ppermute | solution.py:295
  5.0 2.2 %collective-permute-start.2 = (bf16[16,384]{1,0:T(8,128)(2,1)S(1)}, bf16[16,384]{1,0:T(8,128)(2,1)S(1)}, u32[]{:S(2)}, u32[]{:S(2)}) collective-permute-start(bf16[16,384]{1,0:T(8,128)(2,1)S(1)} %turn.1.own_turn), channel_id=1, source_target_pairs={{8,0},{12,4},{16,8},{20,12},{24,16},{28,20},{0,24},{4,28},{9,1},{1... | collective-permute-start | bytes 36872 | tf_op jit(solution)/shard_map/ppermute | solution.py:295
  7.2 0.3 %collective-permute-start.5 = (bf16[16,384]{1,0:T(8,128)(2,1)S(1)}, bf16[16,384]{1,0:T(8,128)(2,1)S(1)}, u32[]{:S(2)}, u32[]{:S(2)}) collective-permute-start(bf16[16,384]{1,0:T(8,128)(2,1)S(1)} %turn.1.own_turn), channel_id=1, source_target_pairs={{4,0},{16,4},{12,8},{24,12},{20,16},{0,20},{28,24},{8,28},{5,1},{1... | collective-permute-start | bytes 36872 | tf_op jit(solution)/shard_map/ppermute | solution.py:295
  8.1 3.2 %own_spectra.1 = (bf16[464,448]{1,0:T(8,128)(2,1)S(1)}, bf16[384,768]{1,0:T(8,128)(2,1)S(1)}, bf16[64,464]{1,0:T(8,128)(2,1)S(1)}, bf16[768,384]{1,0:T(8,128)(2,...) custom-call(s32[1]{0:T(128)S(6)} %copy.14.bins, ...), custom_call_target="tpu_custom_call" | custom-call | flops 100000 | bytes 1000 | tf_op jit(solution)/shard_map/own_spectra/pallas_call | solution.py:335
  11.3 0.2 collective-permute-done.1.far
  11.5 0.3 %collective-permute-done.2.far_turn = bf16[16,384]{1,0:T(8,128)(2,1)S(1)} collective-permute-done((bf16[16,384]{1,0:T(8,128)(2,1)S(1)}, bf16[16,384]{1,0:T(8,128)(2,1)S(1)}, u32[]{:S(2)}, u32[]{:S(2)}) %collective-permute-start.2) | collective-permute-done | bytes 12320 | tf_op jit(solution)/shard_map/ppermute | solution.py:295
  11.8 0.9 %far_spectrum.1.far_packed = bf16[480,768]{1,0:T(8,128)(2,1)S(1)} custom-call(bf16[384,384]{1,0:T(8,128)(2,1)S(1)} %collective-permute-done.1.far, bf16[16,384]{1,0:T(8,128)(2,1)S(1)} %collective-permute-done.2.far_turn, bf16[464,448]{1,0:T(8,128)(2,1)S(1)} %get-tuple-element.30.rows, bf16[384,768]{1,0:T(8,128)(2,1)S(1)} %get-tuple-element.31.cols), custom_call_target="tpu_custom_call" | custom-call | flops 100000 | bytes 1000 | tf_op jit(solution)/shard_map/far_spectrum/pallas_call | solution.py:356
  12.7 0.0 collective-permute-done.halo
  12.7 1.5 %early_strip.1 = (f32[464,768]{1,0:T(8,128)S(1)}, bf16[64,768]{1,0:T(8,128)(2,1)S(1)}) custom-call(bf16[447,384]{1,0:T(8,128)(2,1)S(1)} %collective-permute-done.halo, f32[464,768]{1,0:T(8,128)S(1)} %get-tuple-element.28.own_part, f32[240,384]{1,0:T(8,128)S(1)} %get-tuple-element.29.ctf, bf16[464,448]{1,0:T(8,128)(2,1)S(1)} %get-tuple-element.30.rows, ...), custom_call_target="tpu_custom_call" | custom-call | flops 100000 | bytes 1000 | tf_op jit(solution)/shard_map/early_strip/pallas_call | solution.py:365
  14.2 0.5 %collective-permute-start.4 = (bf16[480,768]{1,0:T(8,128)(2,1)S(1)}, bf16[480,768]{1,0:T(8,128)(2,1)S(1)}, u32[]{:S(2)}, u32[]{:S(2)}) collective-permute-start(bf16[480,768]{1,0:T(8,128)(2,1)S(1)} %far_spectrum.1.far_packed), channel_id=1, source_target_pairs={{4,0},{0,4},{12,8},{8,12},{20,16},{16,20},{28,24},{24,28},{5,1},{1... | collective-permute-start | bytes 2211848 | tf_op jit(solution)/shard_map/ppermute | solution.py:295
  14.7 0.6 %strip.1 = (f32[464,768]{1,0:T(8,128)S(1)}, bf16[64,768]{1,0:T(8,128)(2,1)S(1)}, bf16[64,768]{1,0:T(8,128)(2,1)S(1)}) custom-call(bf16[447,384]{1,0:T(8,128)(2,1)S(1)} %collective-permute-done.halo, f32[464,768]{1,0:T(8,128)S(1)} %get-tuple-element.28.own_part, f32[240,384]{1,0:T(8,128)S(1)} %get-tuple-element.29.ctf, ...), custom_call_target="tpu_custom_call" | custom-call | flops 100000 | bytes 1000 | tf_op jit(solution)/shard_map/strip/pallas_call | solution.py:370
  15.4 0.7 %collective-permute-done.3.near = bf16[384,384]{1,0:T(8,128)(2,1)S(1)} collective-permute-done((bf16[384,384]{1,0:T(8,128)(2,1)}, bf16[384,384]{1,0:T(8,128)(2,1)S(1)}, u32[]{:S(2)}, u32[]{:S(2)}) %collective-permute-start.3) | collective-permute-done | bytes 294944 | tf_op jit(solution)/shard_map/ppermute | solution.py:295
  16.1 0.9 %near_and_far.1 = (bf16[464,768]{1,0:T(8,128)(2,1)S(1)}, bf16[64,768]{1,0:T(8,128)(2,1)S(1)}) custom-call(bf16[384,384]{1,0:T(8,128)(2,1)S(1)} %collective-permute-done.3.near, f32[464,768]{1,0:T(8,128)S(1)} %get-tuple-element.40.micro, bf16[480,768]{1,0:T(8,128)(2,1)S(1)} %far_spectrum.1.far_packed, bf16[464,448]{1,0:T(8,128)(2,1)S(1)} %get-tuple-element.30.rows, ...), custom_call_target="tpu_custom_call" | custom-call | flops 10000000000 | bytes 1000 | tf_op jit(solution)/shard_map/near_and_far/pallas_call | solution.py:373
  17.0 0.0 collective-permute-done.5.near_turn
  17.0 0.0 collective-permute-done.4.late_packed
  17.0 2.3 %match.1 = (f32[64,384]{1,0:T(8,128)}, f32[64,384]{1,0:T(8,128)}, f32[64,384]{1,0:T(8,128)}, f32[64,384]{1,0:T(8,128)}, f32[64,384]{1,0:T(8,128)}) custom-call(f32[464,768]{1,0:T(8,128)S(1)} %get-tuple-element.40.micro, bf16[64,768]{1,0:T(8,128)(2,1)S(1)} %get-tuple-element.41.back_own, bf16[64,768]{1,0:T(8,128)(2,1)S(1)} %get-tuple-element.43.back_far, ...), custom_call_target="tpu_custom_call" | custom-call | flops 100000 | bytes 1000 | tf_op jit(solution)/shard_map/match/pallas_call | solution.py:381
  (1 shorter events, 0.0 us)
Async XLA Ops:
  0.6 12.0 %collective-permute-start = (bf16[447,384]{1,0:T(8,128)(2,1)}, bf16[447,384]{1,0:T(8,128)(2,1)S(1)}, u32[]{:S(2)}, u32[]{:S(2)}) collective-permute-start(bf16[447,384]{1,0:T(8,128)(2,1)} %bitcast.7), channel_id=1, source_target_pairs={{1,0},{2,1},{3,2},{5,4},{6,5},{7,6},{9,8},{10,9},{11,10},{13,12},{... | collective-permute-start | bytes 1029896 | tf_op jit(solution)/shard_map/ppermute | solution.py:323
  2.7 8.8 %collective-permute-start.1 = (bf16[384,384]{1,0:T(8,128)(2,1)}, bf16[384,384]{1,0:T(8,128)(2,1)S(1)}, u32[]{:S(2)}, u32[]{:S(2)}) collective-permute-start(bf16[384,384]{1,0:T(8,128)(2,1)} %bitcast.9), channel_id=1, source_target_pairs={{8,0},{12,4},{16,8},{20,12},{24,16},{28,20},{0,24},{4,28},{9,1},{1... | collective-permute-start | bytes 884744 | tf_op jit(solution)/shard_map/ppermute | solution.py:295
  3.0 13.0 %collective-permute-start.3 = (bf16[384,384]{1,0:T(8,128)(2,1)}, bf16[384,384]{1,0:T(8,128)(2,1)S(1)}, u32[]{:S(2)}, u32[]{:S(2)}) collective-permute-start(bf16[384,384]{1,0:T(8,128)(2,1)} %bitcast.10), channel_id=1, source_target_pairs={{4,0},{16,4},{12,8},{24,12},{20,16},{0,20},{28,24},{8,28},{5,1},{1... | collective-permute-start | bytes 884744 | tf_op jit(solution)/shard_map/ppermute | solution.py:295
  5.0 6.8 %collective-permute-start.2 = (bf16[16,384]{1,0:T(8,128)(2,1)S(1)}, bf16[16,384]{1,0:T(8,128)(2,1)S(1)}, u32[]{:S(2)}, u32[]{:S(2)}) collective-permute-start(bf16[16,384]{1,0:T(8,128)(2,1)S(1)} %turn.1.own_turn), channel_id=1, source_target_pairs={{8,0},{12,4},{16,8},{20,12},{24,16},{28,20},{0,24},{4,28},{9,1},{1... | collective-permute-start | bytes 36872 | tf_op jit(solution)/shard_map/ppermute | solution.py:295
  7.2 9.8 %collective-permute-start.5 = (bf16[16,384]{1,0:T(8,128)(2,1)S(1)}, bf16[16,384]{1,0:T(8,128)(2,1)S(1)}, u32[]{:S(2)}, u32[]{:S(2)}) collective-permute-start(bf16[16,384]{1,0:T(8,128)(2,1)S(1)} %turn.1.own_turn), channel_id=1, source_target_pairs={{4,0},{16,4},{12,8},{24,12},{20,16},{0,20},{28,24},{8,28},{5,1},{1... | collective-permute-start | bytes 36872 | tf_op jit(solution)/shard_map/ppermute | solution.py:295
  14.2 2.8 %collective-permute-start.4 = (bf16[480,768]{1,0:T(8,128)(2,1)S(1)}, bf16[480,768]{1,0:T(8,128)(2,1)S(1)}, u32[]{:S(2)}, u32[]{:S(2)}) collective-permute-start(bf16[480,768]{1,0:T(8,128)(2,1)S(1)} %far_spectrum.1.far_packed), channel_id=1, source_target_pairs={{4,0},{0,4},{12,8},{8,12},{20,16},{16,20},{28,24},{24,28},{5,1},{1... | collective-permute-start | bytes 2211848 | tf_op jit(solution)/shard_map/ppermute | solution.py:295

commit v5 on v4

--- a/solution.py
+++ b/solution.py
@@ -214,10 +214,12 @@
     far_packed,
     early_micro,
     early_back,
+    cols_back,
     micro,
     back_own,
-    back_far,
+    early_corr,
     product,
+    backs,
 ):
     @waits_long(False)
     def _():
@@ -228,27 +230,42 @@
     def _():
         micro[...] = early_micro[...]
         back_own[...] = early_back[...]
-        multiply_back(early_micro, far_packed, rows_back, product, back_far)
+        backs[:MH, :] = early_back[...]
+        multiply_back(early_micro, far_packed, rows_back, product, backs.at[MH:])
+        early_corr[...] = dot(backs[...], cols_back[...])
 
 
 def third_kernel(
-    near, micro, far_packed, rows, cols, rows_back, early_far, near_spectrum, back, product
+    near,
+    micro,
+    far_packed,
+    rows,
+    cols,
+    rows_back,
+    back_own,
+    cols_back,
+    early_corr,
+    near_spectrum,
+    corr,
+    product,
+    backs,
 ):
     @waits_long(False)
     def _():
         store_spectrum(near_spectrum, near, rows, cols)
-        multiply_back(micro, far_packed, rows_back, product, back)
+        backs[:MH, :] = back_own[...]
+        multiply_back(micro, far_packed, rows_back, product, backs.at[MH:])
+        corr[...] = dot(backs[...], cols_back[...])
 
     @waits_long(True)
     def _():
         store_spectrum(near_spectrum, near, rows, cols)
-        back[...] = early_far[...]
+        corr[...] = early_corr[...]
 
 
 def last_kernel(
     micro,
-    back_own,
-    back_far,
+    corr_early,
     near_spectrum,
     late_packed,
     own_turn,
@@ -264,13 +281,11 @@
     products,
     back_all,
 ):
-    back_all[:MH, :] = back_own[...]
-    back_all[MH : 2 * MH, :] = back_far[...]
-    multiply_back(micro, near_spectrum, rows_back, products.at[0], back_all.at[2 * MH : 3 * MH])
-    multiply_back(micro, late_packed, rows_back, products.at[1], back_all.at[3 * MH :])
+    multiply_back(micro, near_spectrum, rows_back, products.at[0], back_all.at[:MH])
+    multiply_back(micro, late_packed, rows_back, products.at[1], back_all.at[MH:])
     scale = 1.0 / (TS * LR * LC)
-    corr_all = dot(back_all[...], cols_back[...]) * scale
-    corrs = [corr_all[step * MH : (step + 1) * MH, :] for step in range(STEPS)]
+    halves = (corr_early[...] * scale, dot(back_all[...], cols_back[...]) * scale)
+    corrs = [half[step * MH : (step + 1) * MH, :] for half in halves for step in range(2)]
     turns = (own_turn[...], far_packed[ROWS:, :HALF], near_turn[...], late_packed[ROWS:, :HALF])
     sums = None
     for corr, turn in zip(corrs, turns):
@@ -367,28 +382,29 @@
     )(*strip_inputs)
     far_packed, early_micro = lax.optimization_barrier((far_packed, early_micro))
     late_packed = along(far_packed, [d ^ 1 for d in range(count)])
-    micro, back_own, early_far = call(
-        strip_kernel, "strip", COST[3], (*strip_types, back_type), [VMEM] * 10, product_scratch
-    )(*strip_inputs, far_packed, early_micro, early_back)
-    near_spectrum, back_far = call(
+    corr_type = jax.ShapeDtypeStruct((2 * MH, TC), f32)
+    corr_scratch = [*product_scratch, pltpu.VMEM((2 * MH, 2 * HALF), bf16)]
+    micro, back_own, early_corr = call(
+        strip_kernel, "strip", COST[3], (*strip_types, corr_type), [VMEM] * 11, corr_scratch
+    )(*strip_inputs, far_packed, early_micro, early_back, cols_back)
+    near_spectrum, corr_early = call(
         third_kernel,
         "near_and_far",
         COST[4],
-        (spectrum_type, back_type),
-        [VMEM] * 7,
-        product_scratch,
-    )(near, micro, far_packed, rows, cols, rows_back, early_far)
+        (spectrum_type, corr_type),
+        [VMEM] * 9,
+        corr_scratch,
+    )(near, micro, far_packed, rows, cols, rows_back, back_own, cols_back, early_corr)
     results = call(
         last_kernel,
         "match",
         COST[5],
         (jax.ShapeDtypeStruct((MH, TC), f32),) * 5,
-        [VMEM] * 10,
-        [pltpu.VMEM((2, ROWS, 2 * HALF), bf16), pltpu.VMEM((STEPS * MH, 2 * HALF), bf16)],
+        [VMEM] * 9,
+        [pltpu.VMEM((2, ROWS, 2 * HALF), bf16), pltpu.VMEM((2 * MH, 2 * HALF), bf16)],
     )(
         micro,
-        back_own,
-        back_far,
+        corr_early,
         near_spectrum,
         late_packed,
         own_turn,

time: 19.5 us -> 19.4 us (level)
  transfers between devices with their start and end apart: 6 -> 6, of which waited for: 3 -> 3; matrix products, arithmetic and copies ran while one was open for 0% -> 0% of each run, Pallas kernels for 37% -> 38%
where the time goes in v5:
time: 19.4 us; the launch traced here: 19.2 us
  Pallas kernels  9.58 us (49%)
  starting transfers between devices  6.66 us (34%)
  between operations  2.01 us (10%)
  waiting for transfers between devices  0.97 us (5%)
    ppermute x5, starting transfers between devices, along(): lax.ppermute(array, 'mic', [(source, place) for place, source in enumerat...  4.57 us
    pallas_call x1, Pallas kernels, body(): call(first_kernel, 'own_spectra', COST[1], (jax.ShapeDtypeStruct(rows_far...  3.18 us
    pallas_call x1, Pallas kernels, body(): call(last_kernel, 'match', COST[5], (jax.ShapeDtypeStruct((MH, TC), f32),...  2.25 us
    ppermute x1, starting transfers between devices, body(): halo = lax.ppermute(strip, 'tile', [(i + 1, i) for i in range(tiles - 1)])  2.1 us
    pallas_call x1, Pallas kernels, body(): call(early_strip_kernel, 'early_strip', COST[3], strip_types, [VMEM] * 7,...  1.49 us
    ppermute x5, waiting for transfers between devices, along(): lax.ppermute(array, 'mic', [(source, place) for place, source in enumerat...  0.97 us
    pallas_call x1, Pallas kernels, body(): call(far_kernel, 'far_spectrum', COST[2], jax.ShapeDtypeStruct((ROWS + ED...  0.9 us
    pallas_call x1, Pallas kernels, body(): call(third_kernel, 'near_and_far', COST[4], (spectrum_type, corr_type), [...  0.89 us
  transfers between devices with their start and end apart: 6, of which 3 were waited for; matrix products, arithmetic and copies ran while one was open for 0% of the time, Pallas kernels for 38%

profile of v5, /device:TPU:27, one launch (start us, length us, event | category | flops | bytes accessed | tf_op | source)
XLA Modules:
  0.0 19.2 jit_solution(12149592109874238988)
XLA Ops:
  0.6 2.1 %collective-permute-start = (bf16[447,384]{1,0:T(8,128)(2,1)}, bf16[447,384]{1,0:T(8,128)(2,1)S(1)}, u32[]{:S(2)}, u32[]{:S(2)}) collective-permute-start(bf16[447,384]{1,0:T(8,128)(2,1)} %bitcast.7), channel_id=1, source_target_pairs={{1,0},{2,1},{3,2},{5,4},{6,5},{7,6},{9,8},{10,9},{11,10},{13,12},{... | collective-permute-start | bytes 1029896 | tf_op jit(solution)/shard_map/ppermute | solution.py:338
  2.7 0.3 %collective-permute-start.1 = (bf16[384,384]{1,0:T(8,128)(2,1)}, bf16[384,384]{1,0:T(8,128)(2,1)S(1)}, u32[]{:S(2)}, u32[]{:S(2)}) collective-permute-start(bf16[384,384]{1,0:T(8,128)(2,1)} %bitcast.9), channel_id=1, source_target_pairs={{8,0},{12,4},{16,8},{20,12},{24,16},{28,20},{0,24},{4,28},{9,1},{1... | collective-permute-start | bytes 884744 | tf_op jit(solution)/shard_map/ppermute | solution.py:310
  3.0 1.2 %collective-permute-start.3 = (bf16[384,384]{1,0:T(8,128)(2,1)}, bf16[384,384]{1,0:T(8,128)(2,1)S(1)}, u32[]{:S(2)}, u32[]{:S(2)}) collective-permute-start(bf16[384,384]{1,0:T(8,128)(2,1)} %bitcast.10), channel_id=1, source_target_pairs={{4,0},{16,4},{12,8},{24,12},{20,16},{0,20},{28,24},{8,28},{5,1},{1... | collective-permute-start | bytes 884744 | tf_op jit(solution)/shard_map/ppermute | solution.py:310
  5.0 2.2 %collective-permute-start.2 = (bf16[16,384]{1,0:T(8,128)(2,1)S(1)}, bf16[16,384]{1,0:T(8,128)(2,1)S(1)}, u32[]{:S(2)}, u32[]{:S(2)}) collective-permute-start(bf16[16,384]{1,0:T(8,128)(2,1)S(1)} %turn.1.own_turn), channel_id=1, source_target_pairs={{8,0},{12,4},{16,8},{20,12},{24,16},{28,20},{0,24},{4,28},{9,1},{1... | collective-permute-start | bytes 36872 | tf_op jit(solution)/shard_map/ppermute | solution.py:310
  7.2 0.3 %collective-permute-start.5 = (bf16[16,384]{1,0:T(8,128)(2,1)S(1)}, bf16[16,384]{1,0:T(8,128)(2,1)S(1)}, u32[]{:S(2)}, u32[]{:S(2)}) collective-permute-start(bf16[16,384]{1,0:T(8,128)(2,1)S(1)} %turn.1.own_turn), channel_id=1, source_target_pairs={{4,0},{16,4},{12,8},{24,12},{20,16},{0,20},{28,24},{8,28},{5,1},{1... | collective-permute-start | bytes 36872 | tf_op jit(solution)/shard_map/ppermute | solution.py:310
  8.1 3.2 %own_spectra.1 = (bf16[464,448]{1,0:T(8,128)(2,1)S(1)}, bf16[384,768]{1,0:T(8,128)(2,1)S(1)}, bf16[64,464]{1,0:T(8,128)(2,1)S(1)}, bf16[768,384]{1,0:T(8,128)(2,...) custom-call(s32[1]{0:T(128)S(6)} %copy.14.bins, ...), custom_call_target="tpu_custom_call" | custom-call | flops 100000 | bytes 1000 | tf_op jit(solution)/shard_map/own_spectra/pallas_call | solution.py:350
  11.3 0.2 collective-permute-done.1.far
  11.5 0.3 %collective-permute-done.2.far_turn = bf16[16,384]{1,0:T(8,128)(2,1)S(1)} collective-permute-done((bf16[16,384]{1,0:T(8,128)(2,1)S(1)}, bf16[16,384]{1,0:T(8,128)(2,1)S(1)}, u32[]{:S(2)}, u32[]{:S(2)}) %collective-permute-start.2) | collective-permute-done | bytes 12320 | tf_op jit(solution)/shard_map/ppermute | solution.py:310
  11.8 0.9 %far_spectrum.1.far_packed = bf16[480,768]{1,0:T(8,128)(2,1)S(1)} custom-call(bf16[384,384]{1,0:T(8,128)(2,1)S(1)} %collective-permute-done.1.far, bf16[16,384]{1,0:T(8,128)(2,1)S(1)} %collective-permute-done.2.far_turn, bf16[464,448]{1,0:T(8,128)(2,1)S(1)} %get-tuple-element.30.rows, bf16[384,768]{1,0:T(8,128)(2,1)S(1)} %get-tuple-element.31.cols), custom_call_target="tpu_custom_call" | custom-call | flops 100000 | bytes 1000 | tf_op jit(solution)/shard_map/far_spectrum/pallas_call | solution.py:371
  12.7 0.0 collective-permute-done.halo
  12.7 1.5 %early_strip.1 = (f32[464,768]{1,0:T(8,128)S(1)}, bf16[64,768]{1,0:T(8,128)(2,1)S(1)}) custom-call(bf16[447,384]{1,0:T(8,128)(2,1)S(1)} %collective-permute-done.halo, f32[464,768]{1,0:T(8,128)S(1)} %get-tuple-element.28.own_part, f32[240,384]{1,0:T(8,128)S(1)} %get-tuple-element.29.ctf, bf16[464,448]{1,0:T(8,128)(2,1)S(1)} %get-tuple-element.30.rows, ...), custom_call_target="tpu_custom_call" | custom-call | flops 100000 | bytes 1000 | tf_op jit(solution)/shard_map/early_strip/pallas_call | solution.py:380
  14.2 0.5 %collective-permute-start.4 = (bf16[480,768]{1,0:T(8,128)(2,1)S(1)}, bf16[480,768]{1,0:T(8,128)(2,1)S(1)}, u32[]{:S(2)}, u32[]{:S(2)}) collective-permute-start(bf16[480,768]{1,0:T(8,128)(2,1)S(1)} %far_spectrum.1.far_packed), channel_id=1, source_target_pairs={{4,0},{0,4},{12,8},{8,12},{20,16},{16,20},{28,24},{24,28},{5,1},{1... | collective-permute-start | bytes 2211848 | tf_op jit(solution)/shard_map/ppermute | solution.py:310
  14.7 0.8 %strip.1 = (f32[464,768]{1,0:T(8,128)S(1)}, bf16[64,768]{1,0:T(8,128)(2,1)S(1)}, f32[128,384]{1,0:T(8,128)S(1)}) custom-call(bf16[447,384]{1,0:T(8,128)(2,1)S(1)} %collective-permute-done.halo, f32[464,768]{1,0:T(8,128)S(1)} %get-tuple-element.28.own_part, f32[240,384]{1,0:T(8,128)S(1)} %get-tuple-element.29.ctf, ...), custom_call_target="tpu_custom_call" | custom-call | flops 100000 | bytes 1000 | tf_op jit(solution)/shard_map/strip/pallas_call | solution.py:387
  15.5 0.5 %collective-permute-done.3.near = bf16[384,384]{1,0:T(8,128)(2,1)S(1)} collective-permute-done((bf16[384,384]{1,0:T(8,128)(2,1)}, bf16[384,384]{1,0:T(8,128)(2,1)S(1)}, u32[]{:S(2)}, u32[]{:S(2)}) %collective-permute-start.3) | collective-permute-done | bytes 294944 | tf_op jit(solution)/shard_map/ppermute | solution.py:310
  16.1 0.9 %near_and_far.1 = (bf16[464,768]{1,0:T(8,128)(2,1)S(1)}, f32[128,384]{1,0:T(8,128)S(1)}) custom-call(bf16[384,384]{1,0:T(8,128)(2,1)S(1)} %collective-permute-done.3.near, f32[464,768]{1,0:T(8,128)S(1)} %get-tuple-element.41.micro, bf16[480,768]{1,0:T(8,128)(2,1)S(1)} %far_spectrum.1.far_packed, bf16[464,448]{1,0:T(8,128)(2,1)S(1)} %get-tuple-element.30.rows, ...), custom_call_target="tpu_custom_call" | custom-call | flops 10000000000 | bytes 1000 | tf_op jit(solution)/shard_map/near_and_far/pallas_call | solution.py:390
  17.0 0.0 collective-permute-done.5.near_turn
  17.0 0.0 collective-permute-done.4.late_packed
  17.0 2.2 %match.1 = (f32[64,384]{1,0:T(8,128)}, f32[64,384]{1,0:T(8,128)}, f32[64,384]{1,0:T(8,128)}, f32[64,384]{1,0:T(8,128)}, f32[64,384]{1,0:T(8,128)}) custom-call(f32[464,768]{1,0:T(8,128)S(1)} %get-tuple-element.41.micro, f32[128,384]{1,0:T(8,128)S(1)} %get-tuple-element.44.corr_early, bf16[464,768]{1,0:T(8,128)(2,1)S(1)} %get-tuple-element.45.near_spectrum, ...), custom_call_target="tpu_custom_call" | custom-call | flops 100000 | bytes 1000 | tf_op jit(solution)/shard_map/match/pallas_call | solution.py:398
  (1 shorter events, 0.0 us)
Async XLA Ops:
  0.6 12.0 %collective-permute-start = (bf16[447,384]{1,0:T(8,128)(2,1)}, bf16[447,384]{1,0:T(8,128)(2,1)S(1)}, u32[]{:S(2)}, u32[]{:S(2)}) collective-permute-start(bf16[447,384]{1,0:T(8,128)(2,1)} %bitcast.7), channel_id=1, source_target_pairs={{1,0},{2,1},{3,2},{5,4},{6,5},{7,6},{9,8},{10,9},{11,10},{13,12},{... | collective-permute-start | bytes 1029896 | tf_op jit(solution)/shard_map/ppermute | solution.py:338
  2.7 8.8 %collective-permute-start.1 = (bf16[384,384]{1,0:T(8,128)(2,1)}, bf16[384,384]{1,0:T(8,128)(2,1)S(1)}, u32[]{:S(2)}, u32[]{:S(2)}) collective-permute-start(bf16[384,384]{1,0:T(8,128)(2,1)} %bitcast.9), channel_id=1, source_target_pairs={{8,0},{12,4},{16,8},{20,12},{24,16},{28,20},{0,24},{4,28},{9,1},{1... | collective-permute-start | bytes 884744 | tf_op jit(solution)/shard_map/ppermute | solution.py:310
  3.0 13.0 %collective-permute-start.3 = (bf16[384,384]{1,0:T(8,128)(2,1)}, bf16[384,384]{1,0:T(8,128)(2,1)S(1)}, u32[]{:S(2)}, u32[]{:S(2)}) collective-permute-start(bf16[384,384]{1,0:T(8,128)(2,1)} %bitcast.10), channel_id=1, source_target_pairs={{4,0},{16,4},{12,8},{24,12},{20,16},{0,20},{28,24},{8,28},{5,1},{1... | collective-permute-start | bytes 884744 | tf_op jit(solution)/shard_map/ppermute | solution.py:310
  5.0 6.8 %collective-permute-start.2 = (bf16[16,384]{1,0:T(8,128)(2,1)S(1)}, bf16[16,384]{1,0:T(8,128)(2,1)S(1)}, u32[]{:S(2)}, u32[]{:S(2)}) collective-permute-start(bf16[16,384]{1,0:T(8,128)(2,1)S(1)} %turn.1.own_turn), channel_id=1, source_target_pairs={{8,0},{12,4},{16,8},{20,12},{24,16},{28,20},{0,24},{4,28},{9,1},{1... | collective-permute-start | bytes 36872 | tf_op jit(solution)/shard_map/ppermute | solution.py:310
  7.2 9.8 %collective-permute-start.5 = (bf16[16,384]{1,0:T(8,128)(2,1)S(1)}, bf16[16,384]{1,0:T(8,128)(2,1)S(1)}, u32[]{:S(2)}, u32[]{:S(2)}) collective-permute-start(bf16[16,384]{1,0:T(8,128)(2,1)S(1)} %turn.1.own_turn), channel_id=1, source_target_pairs={{4,0},{16,4},{12,8},{24,12},{20,16},{0,20},{28,24},{8,28},{5,1},{1... | collective-permute-start | bytes 36872 | tf_op jit(solution)/shard_map/ppermute | solution.py:310
  14.2 2.8 %collective-permute-start.4 = (bf16[480,768]{1,0:T(8,128)(2,1)S(1)}, bf16[480,768]{1,0:T(8,128)(2,1)S(1)}, u32[]{:S(2)}, u32[]{:S(2)}) collective-permute-start(bf16[480,768]{1,0:T(8,128)(2,1)S(1)} %far_spectrum.1.far_packed), channel_id=1, source_target_pairs={{4,0},{0,4},{12,8},{8,12},{20,16},{16,20},{28,24},{24,28},{5,1},{1... | collective-permute-start | bytes 2211848 | tf_op jit(solution)/shard_map/ppermute | solution.py:310

commit v6 on v4

--- a/solution.py
+++ b/solution.py
@@ -65,7 +65,14 @@
 
 
 def store_spectrum(target, template, rows, cols):
-    half_way = dot(rows[:, :TS], template[...]).astype(jnp.bfloat16)
+    finish_spectrum(target, half_spectrum(template, rows), cols)
+
+
+def half_spectrum(template, rows):
+    return dot(rows[:, :TS], template[...]).astype(jnp.bfloat16)
+
+
+def finish_spectrum(target, half_way, cols):
     t_a, t_b, t_d, t_e, t_x, t_y = blocks(dot(half_way, cols[...]))
     target[:PAIRS, :HALF] = (t_a - t_e).astype(jnp.bfloat16)
     target[:PAIRS, HALF:] = (t_b + t_d).astype(jnp.bfloat16)
@@ -125,9 +132,11 @@
         math.sqrt(1.0 - AMPLITUDE * AMPLITUDE) * jnp.sin(phases) + AMPLITUDE * jnp.cos(phases)
     )
     ctf[...] = values * jnp.where(row_ids == 0, 0.5, 1.0)
-    for copy in copies:
+    for copy in copies[:3]:
         copy.wait()
     store_spectrum(spectrum, template, rows, cols)
+    for copy in copies[3:]:
+        copy.wait()
     half_way = dot(rows[:, :MR], strip[...]).astype(jnp.bfloat16)
     own_part[...] = dot(half_way, cols[...])
 
@@ -236,8 +245,9 @@
 ):
     @waits_long(False)
     def _():
-        store_spectrum(near_spectrum, near, rows, cols)
+        near_half = half_spectrum(near, rows)
         multiply_back(micro, far_packed, rows_back, product, back)
+        finish_spectrum(near_spectrum, near_half, cols)
 
     @waits_long(True)
     def _():

time: 19.5 us -> 19.5 us (level)
  no operation moved by 1% of the time
where the time goes in v6:
time: 19.5 us; the launch traced here: 19.3 us
  Pallas kernels  9.55 us (49%)
  starting transfers between devices  6.66 us (34%)
  between operations  2.01 us (10%)
  waiting for transfers between devices  1.09 us (6%)
    ppermute x5, starting transfers between devices, along(): lax.ppermute(array, 'mic', [(source, place) for place, source in enumerat...  4.57 us
    pallas_call x1, Pallas kernels, body(): call(first_kernel, 'own_spectra', COST[1], (jax.ShapeDtypeStruct(rows_far...  3.25 us
    pallas_call x1, Pallas kernels, body(): call(last_kernel, 'match', COST[5], (jax.ShapeDtypeStruct((MH, TC), f32),...  2.33 us
    ppermute x1, starting transfers between devices, body(): halo = lax.ppermute(strip, 'tile', [(i + 1, i) for i in range(tiles - 1)])  2.1 us
    pallas_call x1, Pallas kernels, body(): call(early_strip_kernel, 'early_strip', COST[3], strip_types, [VMEM] * 7,...  1.49 us
    ppermute x5, waiting for transfers between devices, along(): lax.ppermute(array, 'mic', [(source, place) for place, source in enumerat...  1.09 us
    pallas_call x1, Pallas kernels, body(): call(far_kernel, 'far_spectrum', COST[2], jax.ShapeDtypeStruct((ROWS + ED...  0.9 us
    pallas_call x1, Pallas kernels, body(): call(third_kernel, 'near_and_far', COST[4], (spectrum_type, back_type), [...  0.89 us
  transfers between devices with their start and end apart: 6, of which 3 were waited for; matrix products, arithmetic and copies ran while one was open for 0% of the time, Pallas kernels for 37%

profile of v6, /device:TPU:27, one launch (start us, length us, event | category | flops | bytes accessed | tf_op | source)
XLA Modules:
  0.0 19.3 jit_solution(1300032747835078153)
XLA Ops:
  0.6 2.1 %collective-permute-start = (bf16[447,384]{1,0:T(8,128)(2,1)}, bf16[447,384]{1,0:T(8,128)(2,1)S(1)}, u32[]{:S(2)}, u32[]{:S(2)}) collective-permute-start(bf16[447,384]{1,0:T(8,128)(2,1)} %bitcast.7), channel_id=1, source_target_pairs={{1,0},{2,1},{3,2},{5,4},{6,5},{7,6},{9,8},{10,9},{11,10},{13,12},{... | collective-permute-start | bytes 1029896 | tf_op jit(solution)/shard_map/ppermute | solution.py:333
  2.7 0.3 %collective-permute-start.1 = (bf16[384,384]{1,0:T(8,128)(2,1)}, bf16[384,384]{1,0:T(8,128)(2,1)S(1)}, u32[]{:S(2)}, u32[]{:S(2)}) collective-permute-start(bf16[384,384]{1,0:T(8,128)(2,1)} %bitcast.9), channel_id=1, source_target_pairs={{8,0},{12,4},{16,8},{20,12},{24,16},{28,20},{0,24},{4,28},{9,1},{1... | collective-permute-start | bytes 884744 | tf_op jit(solution)/shard_map/ppermute | solution.py:305
  3.0 1.2 %collective-permute-start.3 = (bf16[384,384]{1,0:T(8,128)(2,1)}, bf16[384,384]{1,0:T(8,128)(2,1)S(1)}, u32[]{:S(2)}, u32[]{:S(2)}) collective-permute-start(bf16[384,384]{1,0:T(8,128)(2,1)} %bitcast.10), channel_id=1, source_target_pairs={{4,0},{16,4},{12,8},{24,12},{20,16},{0,20},{28,24},{8,28},{5,1},{1... | collective-permute-start | bytes 884744 | tf_op jit(solution)/shard_map/ppermute | solution.py:305
  5.0 2.2 %collective-permute-start.2 = (bf16[16,384]{1,0:T(8,128)(2,1)S(1)}, bf16[16,384]{1,0:T(8,128)(2,1)S(1)}, u32[]{:S(2)}, u32[]{:S(2)}) collective-permute-start(bf16[16,384]{1,0:T(8,128)(2,1)S(1)} %turn.1.own_turn), channel_id=1, source_target_pairs={{8,0},{12,4},{16,8},{20,12},{24,16},{28,20},{0,24},{4,28},{9,1},{1... | collective-permute-start | bytes 36872 | tf_op jit(solution)/shard_map/ppermute | solution.py:305
  7.2 0.3 %collective-permute-start.5 = (bf16[16,384]{1,0:T(8,128)(2,1)S(1)}, bf16[16,384]{1,0:T(8,128)(2,1)S(1)}, u32[]{:S(2)}, u32[]{:S(2)}) collective-permute-start(bf16[16,384]{1,0:T(8,128)(2,1)S(1)} %turn.1.own_turn), channel_id=1, source_target_pairs={{4,0},{16,4},{12,8},{24,12},{20,16},{0,20},{28,24},{8,28},{5,1},{1... | collective-permute-start | bytes 36872 | tf_op jit(solution)/shard_map/ppermute | solution.py:305
  8.1 3.2 %own_spectra.1 = (bf16[464,448]{1,0:T(8,128)(2,1)S(1)}, bf16[384,768]{1,0:T(8,128)(2,1)S(1)}, bf16[64,464]{1,0:T(8,128)(2,1)S(1)}, bf16[768,384]{1,0:T(8,128)(2,...) custom-call(s32[1]{0:T(128)S(6)} %copy.14.bins, ...), custom_call_target="tpu_custom_call" | custom-call | flops 100000 | bytes 1000 | tf_op jit(solution)/shard_map/own_spectra/pallas_call | solution.py:345
  11.4 0.1 collective-permute-done.1.far
  11.5 0.3 %collective-permute-done.2.far_turn = bf16[16,384]{1,0:T(8,128)(2,1)S(1)} collective-permute-done((bf16[16,384]{1,0:T(8,128)(2,1)S(1)}, bf16[16,384]{1,0:T(8,128)(2,1)S(1)}, u32[]{:S(2)}, u32[]{:S(2)}) %collective-permute-start.2) | collective-permute-done | bytes 12320 | tf_op jit(solution)/shard_map/ppermute | solution.py:305
  11.8 0.9 %far_spectrum.1.far_packed = bf16[480,768]{1,0:T(8,128)(2,1)S(1)} custom-call(bf16[384,384]{1,0:T(8,128)(2,1)S(1)} %collective-permute-done.1.far, bf16[16,384]{1,0:T(8,128)(2,1)S(1)} %collective-permute-done.2.far_turn, bf16[464,448]{1,0:T(8,128)(2,1)S(1)} %get-tuple-element.30.rows, bf16[384,768]{1,0:T(8,128)(2,1)S(1)} %get-tuple-element.31.cols), custom_call_target="tpu_custom_call" | custom-call | flops 100000 | bytes 1000 | tf_op jit(solution)/shard_map/far_spectrum/pallas_call | solution.py:366
  12.7 0.0 collective-permute-done.halo
  12.7 1.5 %early_strip.1 = (f32[464,768]{1,0:T(8,128)S(1)}, bf16[64,768]{1,0:T(8,128)(2,1)S(1)}) custom-call(bf16[447,384]{1,0:T(8,128)(2,1)S(1)} %collective-permute-done.halo, f32[464,768]{1,0:T(8,128)S(1)} %get-tuple-element.28.own_part, f32[240,384]{1,0:T(8,128)S(1)} %get-tuple-element.29.ctf, bf16[464,448]{1,0:T(8,128)(2,1)S(1)} %get-tuple-element.30.rows, ...), custom_call_target="tpu_custom_call" | custom-call | flops 100000 | bytes 1000 | tf_op jit(solution)/shard_map/early_strip/pallas_call | solution.py:375
  14.2 0.5 %collective-permute-start.4 = (bf16[480,768]{1,0:T(8,128)(2,1)S(1)}, bf16[480,768]{1,0:T(8,128)(2,1)S(1)}, u32[]{:S(2)}, u32[]{:S(2)}) collective-permute-start(bf16[480,768]{1,0:T(8,128)(2,1)S(1)} %far_spectrum.1.far_packed), channel_id=1, source_target_pairs={{4,0},{0,4},{12,8},{8,12},{20,16},{16,20},{28,24},{24,28},{5,1},{1... | collective-permute-start | bytes 2211848 | tf_op jit(solution)/shard_map/ppermute | solution.py:305
  14.7 0.6 %strip.1 = (f32[464,768]{1,0:T(8,128)S(1)}, bf16[64,768]{1,0:T(8,128)(2,1)S(1)}, bf16[64,768]{1,0:T(8,128)(2,1)S(1)}) custom-call(bf16[447,384]{1,0:T(8,128)(2,1)S(1)} %collective-permute-done.halo, f32[464,768]{1,0:T(8,128)S(1)} %get-tuple-element.28.own_part, f32[240,384]{1,0:T(8,128)S(1)} %get-tuple-element.29.ctf, ...), custom_call_target="tpu_custom_call" | custom-call | flops 100000 | bytes 1000 | tf_op jit(solution)/shard_map/strip/pallas_call | solution.py:380
  15.4 0.7 %collective-permute-done.3.near = bf16[384,384]{1,0:T(8,128)(2,1)S(1)} collective-permute-done((bf16[384,384]{1,0:T(8,128)(2,1)}, bf16[384,384]{1,0:T(8,128)(2,1)S(1)}, u32[]{:S(2)}, u32[]{:S(2)}) %collective-permute-start.3) | collective-permute-done | bytes 294944 | tf_op jit(solution)/shard_map/ppermute | solution.py:305
  16.1 0.9 %near_and_far.1 = (bf16[464,768]{1,0:T(8,128)(2,1)S(1)}, bf16[64,768]{1,0:T(8,128)(2,1)S(1)}) custom-call(bf16[384,384]{1,0:T(8,128)(2,1)S(1)} %collective-permute-done.3.near, f32[464,768]{1,0:T(8,128)S(1)} %get-tuple-element.40.micro, bf16[480,768]{1,0:T(8,128)(2,1)S(1)} %far_spectrum.1.far_packed, bf16[464,448]{1,0:T(8,128)(2,1)S(1)} %get-tuple-element.30.rows, ...), custom_call_target="tpu_custom_call" | custom-call | flops 10000000000 | bytes 1000 | tf_op jit(solution)/shard_map/near_and_far/pallas_call | solution.py:383
  17.0 0.0 collective-permute-done.5.near_turn
  17.0 0.0 collective-permute-done.4.late_packed
  17.0 2.3 %match.1 = (f32[64,384]{1,0:T(8,128)}, f32[64,384]{1,0:T(8,128)}, f32[64,384]{1,0:T(8,128)}, f32[64,384]{1,0:T(8,128)}, f32[64,384]{1,0:T(8,128)}) custom-call(f32[464,768]{1,0:T(8,128)S(1)} %get-tuple-element.40.micro, bf16[64,768]{1,0:T(8,128)(2,1)S(1)} %get-tuple-element.41.back_own, bf16[64,768]{1,0:T(8,128)(2,1)S(1)} %get-tuple-element.43.back_far, ...), custom_call_target="tpu_custom_call" | custom-call | flops 100000 | bytes 1000 | tf_op jit(solution)/shard_map/match/pallas_call | solution.py:391
  (1 shorter events, 0.0 us)
Async XLA Ops:
  0.6 12.0 %collective-permute-start = (bf16[447,384]{1,0:T(8,128)(2,1)}, bf16[447,384]{1,0:T(8,128)(2,1)S(1)}, u32[]{:S(2)}, u32[]{:S(2)}) collective-permute-start(bf16[447,384]{1,0:T(8,128)(2,1)} %bitcast.7), channel_id=1, source_target_pairs={{1,0},{2,1},{3,2},{5,4},{6,5},{7,6},{9,8},{10,9},{11,10},{13,12},{... | collective-permute-start | bytes 1029896 | tf_op jit(solution)/shard_map/ppermute | solution.py:333
  2.7 8.8 %collective-permute-start.1 = (bf16[384,384]{1,0:T(8,128)(2,1)}, bf16[384,384]{1,0:T(8,128)(2,1)S(1)}, u32[]{:S(2)}, u32[]{:S(2)}) collective-permute-start(bf16[384,384]{1,0:T(8,128)(2,1)} %bitcast.9), channel_id=1, source_target_pairs={{8,0},{12,4},{16,8},{20,12},{24,16},{28,20},{0,24},{4,28},{9,1},{1... | collective-permute-start | bytes 884744 | tf_op jit(solution)/shard_map/ppermute | solution.py:305
  3.0 13.0 %collective-permute-start.3 = (bf16[384,384]{1,0:T(8,128)(2,1)}, bf16[384,384]{1,0:T(8,128)(2,1)S(1)}, u32[]{:S(2)}, u32[]{:S(2)}) collective-permute-start(bf16[384,384]{1,0:T(8,128)(2,1)} %bitcast.10), channel_id=1, source_target_pairs={{4,0},{16,4},{12,8},{24,12},{20,16},{0,20},{28,24},{8,28},{5,1},{1... | collective-permute-start | bytes 884744 | tf_op jit(solution)/shard_map/ppermute | solution.py:305
  5.0 6.8 %collective-permute-start.2 = (bf16[16,384]{1,0:T(8,128)(2,1)S(1)}, bf16[16,384]{1,0:T(8,128)(2,1)S(1)}, u32[]{:S(2)}, u32[]{:S(2)}) collective-permute-start(bf16[16,384]{1,0:T(8,128)(2,1)S(1)} %turn.1.own_turn), channel_id=1, source_target_pairs={{8,0},{12,4},{16,8},{20,12},{24,16},{28,20},{0,24},{4,28},{9,1},{1... | collective-permute-start | bytes 36872 | tf_op jit(solution)/shard_map/ppermute | solution.py:305
  7.2 9.8 %collective-permute-start.5 = (bf16[16,384]{1,0:T(8,128)(2,1)S(1)}, bf16[16,384]{1,0:T(8,128)(2,1)S(1)}, u32[]{:S(2)}, u32[]{:S(2)}) collective-permute-start(bf16[16,384]{1,0:T(8,128)(2,1)S(1)} %turn.1.own_turn), channel_id=1, source_target_pairs={{4,0},{16,4},{12,8},{24,12},{20,16},{0,20},{28,24},{8,28},{5,1},{1... | collective-permute-start | bytes 36872 | tf_op jit(solution)/shard_map/ppermute | solution.py:305
  14.2 2.8 %collective-permute-start.4 = (bf16[480,768]{1,0:T(8,128)(2,1)S(1)}, bf16[480,768]{1,0:T(8,128)(2,1)S(1)}, u32[]{:S(2)}, u32[]{:S(2)}) collective-permute-start(bf16[480,768]{1,0:T(8,128)(2,1)S(1)} %far_spectrum.1.far_packed), channel_id=1, source_target_pairs={{4,0},{0,4},{12,8},{8,12},{20,16},{16,20},{28,24},{24,28},{5,1},{1... | collective-permute-start | bytes 2211848 | tf_op jit(solution)/shard_map/ppermute | solution.py:305
